TPU v7x, 256 devices: a whole 4x4x8 slice. The times are simulated.
256 devices in a mesh: prod: 32 (over y, z), week: 8 (over x, core).
Axes of the slice: x: 4, y: 4, z: 8, core: 2. Of those that a mesh axis runs over, the one named last changes fastest.
Arguments:
- regressors: bfloat16 [32, 512, 49152], P(None, 'week', 'prod')
- weights: int32 [512, 49152], P('week', 'prod'), may hold values from 1 to 4
- first_week: int32 [49152], P('prod'), may hold values from 0 to 511, as said below
- last_week: int32 [49152], P('prod'), may hold values from 0 to 511, as said below
Outputs:
- demeaned: bfloat16 [32, 512, 49152], P(None, 'week', 'prod')
- gram: float32 [32, 32], replicated
Inputs may be any that keep to these rules, and one draw needn't show every extreme that they name: `first_week`: product 0 is active in every week, product 1 only in week 0, the last product only in week 512 - 1. last_week[p] >= first_week[p] for every product p.
All inputs are finite; a program needn't handle non-finite values.
Results may differ from a plain program's by a relative error of at most 0.001.
Values sent between devices are 32-bit elements; how exact they have to be, the bound alone decides.
A program may use at most 128 MiB of HBM per device.

v0:
```python
import jax
import jax.numpy as jnp
from jax import lax
from jax.sharding import PartitionSpec as P

SWEEPS = 4


def product_means(numer, product_total):
    return lax.psum(numer, "week") / product_total[None, :]


def week_means(numer, week_total):
    return lax.psum(numer, "prod") / week_total[None, :]


def per_device(regressors, weights, first_week, last_week):
    count_cols, week_rows, prod_cols = regressors.shape
    week_ids = lax.axis_index("week") * week_rows + jnp.arange(week_rows, dtype=jnp.int32)
    active = (week_ids[:, None] >= first_week[None, :]) & (week_ids[:, None] <= last_week[None, :])
    cell_weight = jnp.where(active, weights.astype(jnp.float32), jnp.float32(0.0))
    product_total = lax.psum(jnp.sum(cell_weight, axis=0), "week")
    week_total = lax.psum(jnp.sum(cell_weight, axis=1), "prod")
    values = regressors.astype(jnp.float32)
    field = values
    for sweep in range(SWEEPS):
        product_mean = product_means(jnp.sum(field * cell_weight[None], axis=1), product_total)
        field = field - product_mean[:, None, :]
        week_mean = week_means(jnp.sum(field * cell_weight[None], axis=2), week_total)
        field = field - week_mean[:, :, None]
    demeaned = jnp.where(active[None], field, jnp.float32(0.0))
    weighted = demeaned * cell_weight[None]
    local_gram = jnp.einsum("kwp,lwp->kl", weighted, demeaned, precision=lax.Precision.HIGHEST)
    gram_total, weight_total = lax.psum((local_gram, jnp.sum(cell_weight)), ("prod", "week"))
    return (demeaned.astype(jnp.bfloat16), gram_total / weight_total)


def solution(mesh):
    return jax.shard_map(
        per_device,
        mesh=mesh,
        in_specs=(P(None, "week", "prod"), P("week", "prod"), P("prod"), P("prod")),
        out_specs=(P(None, "week", "prod"), P()),
        check_vma=False,
    )
```

profile of v0, /device:TPU:1, one launch (start us, length us, event | category | flops | bytes accessed | tf_op | source)
XLA Modules:
  0.0 989.2 jit_solution(14342572286729453269)
XLA Ops:
  7.2 0.0 all-reduce.7.cloned.1.call-start
  7.2 1.8 fusion.23
  9.0 5.0 fusion.12
  14.0 0.0 all-reduce.7.cloned.1.call-update
  14.1 0.0 all-reduce.9.cloned.1.call-start
  14.1 15.2 %psum.85 = f32[1536]{0:T(1024)S(1)} all-reduce(f32[1536]{0:T(1024)S(1)} %get-tuple-element.4), channel_id=1, replica_groups=mesh['prod'=32,'week'=8] {'week'}, use_global_device_ids=true, to_apply=%region_3.4 | all-reduce | flops 1536 | bytes 12288 | tf_op jit(solution)/shard_map/psum | solution.py:22
  29.4 51.3 %all-reduce.7.cloned.1.call-done = f32[32,1536]{1,0:T(8,128)} async-done(((f32[32,1536]{1,0:T(8,128)}), f32[32,1536]{1,0:T(8,128)}) %all-reduce.7.cloned.1.call-update) | async-done | bytes 196624 | tf_op jit(solution)/shard_map/psum | solution.py:10
  80.7 0.9 broadcast_divide_fusion.3
  81.6 4.5 fusion.11
  86.2 115.6 %all-reduce.1 = (f32[32,64]{1,0:T(8,128)S(1)}, f32[64]{0:T(128)S(1)}) all-reduce(f32[32,64]{1,0:T(8,128)S(1)} %fusion.11, f32[64]{0:T(128)S(1)} %get-tuple-element.3), channel_id=1, replica_groups=mesh['prod'=32,'week'=8] {'prod'}, use_global_device_ids=true, to_apply=%region_5.6 | all-reduce | flops 2112 | bytes 16896 | tf_op jit(solution)/shard_map/psum | solution.py:14
  201.8 6.6 fusion.10
  208.4 0.0 all-reduce.11.cloned.1.call-start
  208.5 83.5 %all-reduce.9.cloned.1.call-done = f32[32,1536]{1,0:T(8,128)} async-done(((f32[32,1536]{1,0:T(8,128)}), f32[32,1536]{1,0:T(8,128)}) %all-reduce.9.cloned.1.call-update) | async-done | bytes 196624 | tf_op jit(solution)/shard_map/psum | solution.py:10
  292.0 0.9 broadcast_divide_fusion.2
  293.0 5.2 fusion.9
  298.2 115.8 %psum.89 = f32[32,64]{1,0:T(8,128)S(1)} all-reduce(f32[32,64]{1,0:T(8,128)S(1)} %fusion.9), channel_id=1, replica_groups=mesh['prod'=32,'week'=8] {'prod'}, use_global_device_ids=true, to_apply=%region_11.12 | all-reduce | flops 2048 | bytes 16384 | tf_op jit(solution)/shard_map/psum | solution.py:14
  414.0 6.7 fusion.8
  420.7 0.2 all-reduce.13.cloned.1.call-start
  421.0 83.3 %all-reduce.11.cloned.1.call-done = f32[32,1536]{1,0:T(8,128)} async-done(((f32[32,1536]{1,0:T(8,128)}), f32[32,1536]{1,0:T(8,128)}) %all-reduce.11.cloned.1.call-update) | async-done | bytes 196624 | tf_op jit(solution)/shard_map/psum | solution.py:10
  504.3 0.9 broadcast_divide_fusion.1
  505.2 6.0 multiply_reduce_fusion.2
  511.2 115.6 %psum.91 = f32[32,64]{1,0:T(8,128)S(1)} all-reduce(f32[32,64]{1,0:T(8,128)S(1)} %multiply_reduce_fusion.2), channel_id=1, replica_groups=mesh['prod'=32,'week'=8] {'prod'}, use_global_device_ids=true, to_apply=%region_15.16 | all-reduce | flops 2048 | bytes 16384 | tf_op jit(solution)/shard_map/psum | solution.py:14
  626.9 8.2 multiply_reduce_fusion.1
  635.1 0.1 compare_and_fusion
  635.3 83.4 %all-reduce.13.cloned.1.call-done = f32[32,1536]{1,0:T(8,128)} async-done(((f32[32,1536]{1,0:T(8,128)}), f32[32,1536]{1,0:T(8,128)}) %all-reduce.13.cloned.1.call-update) | async-done | bytes 196624 | tf_op jit(solution)/shard_map/psum | solution.py:10
  718.6 0.9 broadcast_divide_fusion
  719.6 7.1 multiply_reduce_fusion
  726.7 115.6 %psum.93 = f32[32,64]{1,0:T(8,128)S(1)} all-reduce(f32[32,64]{1,0:T(8,128)S(1)} %multiply_reduce_fusion), channel_id=1, replica_groups=mesh['prod'=32,'week'=8] {'prod'}, use_global_device_ids=true, to_apply=%region_19.20 | all-reduce | flops 2048 | bytes 16384 | tf_op jit(solution)/shard_map/psum | solution.py:14
  842.3 14.0 %broadcast_multiply_fusion = (f32[32,64,1536]{2,1,0:T(8,128)S(1)}, bf16[32,64,1536]{2,1,0:T(8,128)(2,1)}, f32[32,64,1536]{2,1,0:T(8,128)}) fusion(f32[64,1536]{1,0:T(8,128)S(1)} %get-tuple-element.9, f32[32,64]{1,0:T(8,128)S(1)} %broadcast_divide_fusion.5, f32[32,1536]{1,0:T(8,128)S(1)} %broadcast_divide_fusion, f32[32,64]{1,0:T(8,128)S(1)} %broadcast_divide_fusion.6, ...), kind=kLoop, calls=%fused_computation.23 | loop fusion | flops 37748736 | bytes 39059456 | tf_op jit(solution)/shard_map/mul | solution.py:32
  856.4 24.0 %fusion.17 = f32[32,32]{1,0:T(8,128)S(1)} fusion(f32[32,64,1536]{2,1,0:T(8,128)} %get-tuple-element.12, f32[32,64,1536]{2,1,0:T(8,128)S(1)} %get-tuple-element.10), kind=kOutput, calls=%fused_computation.24 | convolution fusion | flops 1207959552 | bytes 25169920 | tf_op jit(solution)/shard_map/kwp,lwp->kl/dot_general | solution.py:33
  880.4 101.0 %all-reduce = (f32[32,32]{1,0:T(8,128)S(1)}, f32[]{:T(128)}) all-reduce(f32[32,32]{1,0:T(8,128)S(1)} %fusion.17, f32[]{:T(128)} %get-tuple-element.2), channel_id=1, replica_groups=mesh['prod'=32,'week'=8] {'prod','week'}, use_global_device_ids=true, to_apply=%region_20.21 | all-reduce | flops 1025 | bytes 8200 | tf_op jit(solution)/shard_map/psum | solution.py:34
  981.3 1.3 broadcast_divide_fusion.4
  (12 shorter events, 0.1 us)
Async XLA Ops:
  7.2 73.5 %all-reduce.7.cloned.1.call-start = ((), (), s32[]{:S(2)}) async-start(), calls=%async_computation | async-start | bytes 393216 | tf_op jit(solution)/shard_map/psum | solution.py:10
  14.1 277.9 %all-reduce.9.cloned.1.call-start = ((), (), s32[]{:S(2)}) async-start(), calls=%async_computation.1 | async-start | bytes 393216 | tf_op jit(solution)/shard_map/psum | solution.py:10
  208.4 295.8 %all-reduce.11.cloned.1.call-start = ((), (), s32[]{:S(2)}) async-start(), calls=%async_computation.2 | async-start | bytes 393216 | tf_op jit(solution)/shard_map/psum | solution.py:10
  298.2 336.9 %copy-start = (s32[1536]{0:T(1024)S(1)}, s32[1536]{0:T(1024)}, u32[]{:S(2)}) copy-start(s32[1536]{0:T(1024)} %param.7) | copy-start | bytes 18436
  298.2 336.9 %copy-start.1 = (s32[1536]{0:T(1024)S(1)}, s32[1536]{0:T(1024)}, u32[]{:S(2)}) copy-start(s32[1536]{0:T(1024)} %param.6) | copy-start | bytes 18436
  420.7 297.9 %all-reduce.13.cloned.1.call-start = ((), (), s32[]{:S(2)}) async-start(), calls=%async_computation.3 | async-start | bytes 393216 | tf_op jit(solution)/shard_map/psum | solution.py:10
Sparse Core Ops, SparseCore 0:
  14.2 66.4 all-reduce.6
  208.6 83.3 all-reduce.8
  420.8 83.4 all-reduce.10
  635.2 83.3 all-reduce.12
where the time goes:
time: 990 us; the launch traced here: 989 us
  blocking collectives  579 us (58%)
  waiting for transfers between devices  302 us (31%)
  other arithmetic  70.5 us (7%)
  matrix products  24 us (2%)
  between operations  13.8 us (1%)
    psum x4, blocking collectives, week_means(): return lax.psum(numer, 'prod') / week_total[None, :]  463 us
    psum x4, waiting for transfers between devices, product_means(): return lax.psum(numer, 'week') / product_total[None, :]  302 us
    psum x1, blocking collectives, per_device(): lax.psum((local_gram, jnp.sum(cell_weight)), ('prod', 'week'))  101 us
    reduce_sum x4, other arithmetic, per_device(): jnp.sum(field * cell_weight[None], axis=1)  26.6 us
    dot_general x1, matrix products, per_device(): jnp.einsum('kwp,lwp->kl', weighted, demeaned, precision=lax.Precision.HIG...  24 us
    reduce_sum x4, other arithmetic, per_device(): jnp.sum(field * cell_weight[None], axis=2)  22.9 us
  transfers between devices with their start and end apart: 4, of which 4 were waited for; matrix products, arithmetic and copies ran while one was open for 0% of the time, Pallas kernels for 0%

commit v1 on v0

v1 whole, which is shorter than its diff:
```python
import functools

import jax
import jax.numpy as jnp
from jax import lax
from jax.experimental import pallas as pl
from jax.experimental.pallas import tpu as pltpu
from jax.sharding import PartitionSpec as P

MESH = pl.DeviceIdType.MESH
F32 = jnp.float32
BF16 = jnp.bfloat16
HI = lax.Precision.HIGHEST
NT = (((1,), (1,)), ((), ()))
NN = (((1,), (0,)), ((), ()))

K = 32
WK = 64
PD = 1536
NW = 8
NX = 4
NP = 32
WEEKS = NW * WK
LC = 384
HALF = PD // 2


def split3(v):
    hi = v.astype(BF16)
    r = v - hi.astype(F32)
    mid = r.astype(BF16)
    lo = (r - mid.astype(F32)).astype(BF16)
    return hi, mid, lo


def loop(lo, hi, body):
    def step(i, carry):
        body(i)
        return carry

    lax.fori_loop(lo, hi, step, 0)


def effects_kernel(
    x_hbm, weights, first, last,
    pe4_out, we4_out, gram_out,
    x, wfull, wb, pt_all, pt, ps_stage, ps_recv, pe1_chunks, pe1,
    b_pack, b_recv, b_all, m_stage, m_recv, mm,
    q_buf, u_buf, r_pack, r_week, r_prod, we_buf,
    x_sem, pt_s, pt_r, ps_s, ps_r, pe_s, pe_r, wx_s, wx_r, wc_s, wc_r,
    b_s, b_r, ba_s, ba_r, ms_s, ms_r, ma_s, ma_r, mx_s, mx_r, mc_s, mc_r,
    rw_s, rw_r, rp_s, rp_r,
):
    w = lax.axis_index("week")
    p = lax.axis_index("prod")
    xi = w // 2
    core = lax.rem(w, 2)
    sib = xi * 2 + (1 - core)

    def week_peer(d):
        return lax.rem(w + d, NW)

    def prod_peer(d):
        return lax.rem(p + d, NP)

    def x_peer(d):
        return lax.rem(xi + d, NX) * 2 + core

    def x_from(d):
        return lax.rem(xi + NX - d, NX) * 2 + core

    def to_week(src, dst, ssem, rsem, q):
        return pltpu.make_async_remote_copy(
            src_ref=src, dst_ref=dst, send_sem=ssem, recv_sem=rsem,
            device_id={"week": q}, device_id_type=MESH,
        )

    def to_prod(src, dst, ssem, rsem, q):
        return pltpu.make_async_remote_copy(
            src_ref=src, dst_ref=dst, send_sem=ssem, recv_sem=rsem,
            device_id={"prod": q}, device_id_type=MESH,
        )

    def x_copy(c):
        rows = pl.ds(c * 8, 8)
        return pltpu.make_async_copy(x_hbm.at[rows], x.at[rows], x_sem.at[c])

    for c in range(4):
        x_copy(c).start()

    barrier = pltpu.get_barrier_semaphore()

    def greet_week(d):
        pl.semaphore_signal(barrier, inc=1, device_id={"week": week_peer(d)}, device_id_type=MESH)

    def greet_prod(d):
        pl.semaphore_signal(barrier, inc=1, device_id={"prod": prod_peer(d)}, device_id_type=MESH)

    loop(1, NW, greet_week)
    loop(1, NP, greet_prod)

    wown = wfull.at[w]
    ids = w * WK + lax.broadcasted_iota(jnp.int32, (WK, PD), 0)
    live = (ids >= first[...]) & (ids <= last[...])
    cell = jnp.where(live, weights[...].astype(F32), 0.0)
    wown[...] = cell
    pt_all[w] = jnp.sum(cell, axis=0, keepdims=True)

    def ps_group(g):
        x_copy(g).wait()

        def one(j):
            k = g * 8 + j
            for c in range(PD // LC):
                lanes = slice(c * LC, (c + 1) * LC)
                weighted = x[k, :, lanes].astype(F32) * wfull[w, :, lanes]
                half, off = c // 2, (c % 2) * LC
                ps_stage[g * 2 + half, pl.ds(j, 1), off:off + LC] = jnp.sum(weighted, axis=0, keepdims=True)

        loop(0, 8, one)

    loop(0, 4, ps_group)

    pl.semaphore_wait(barrier, NW - 1 + NP - 1)

    def pt_copy(d):
        return to_week(pt_all.at[w], pt_all.at[w], pt_s.at[d], pt_r.at[d], week_peer(d))

    def pt_arrived(d):
        return to_week(pt_all.at[w], pt_all.at[lax.rem(w + NW - d, NW)], pt_s.at[d], pt_r.at[d], week_peer(d))

    def ps_copy(d):
        q = week_peer(d)
        return to_week(ps_stage.at[q], ps_recv.at[d], ps_s.at[d], ps_r.at[d], q)

    def send_ps(d):
        pt_copy(d).start()
        ps_copy(d).start()

    loop(1, NW, send_ps)

    def wx_copy(d):
        return to_week(wfull.at[w], wfull.at[w], wx_s.at[d], wx_r.at[d], x_peer(d))

    def wx_arrived(d):
        return to_week(wfull.at[w], wfull.at[x_from(d)], wx_s.at[d], wx_r.at[d], x_peer(d))

    def wc_copy(d):
        slot = x_from(d)
        return to_week(wfull.at[slot], wfull.at[slot], wc_s.at[d], wc_r.at[d], sib)

    def wc_arrived(d):
        slot = x_from(d)
        slot = slot + 1 - 2 * core
        return to_week(wfull.at[slot], wfull.at[slot], wc_s.at[d], wc_r.at[d], sib)

    for d in (1, 3, 2):
        wx_copy(d).start()
    wc_copy(0).start()

    def wait_ps(d):
        pt_arrived(d).wait_recv()
        ps_copy(d).wait_recv()

    loop(1, NW, wait_ps)
    pt[...] = jnp.sum(pt_all[...], axis=0)
    total = ps_stage[w]
    for d in range(1, NW):
        total = total + ps_recv[d]
    own_half = pl.ds(pl.multiple_of(lax.rem(w, 2) * HALF, HALF), HALF)
    pe1_chunks[w] = total / pt[:, own_half]

    def pe_copy(d):
        return to_week(pe1_chunks.at[w], pe1_chunks.at[w], pe_s.at[d], pe_r.at[d], week_peer(d))

    def pe_arrived(d):
        return to_week(pe1_chunks.at[w], pe1_chunks.at[lax.rem(w + NW - d, NW)], pe_s.at[d], pe_r.at[d], week_peer(d))

    loop(1, NW, lambda d: pe_copy(d).start())
    loop(1, NW, lambda d: pe_arrived(d).wait_recv())
    for r in range(NW):
        pe1[(r // 2) * 8:(r // 2) * 8 + 8, (r % 2) * HALF:(r % 2 + 1) * HALF] = pe1_chunks[r]

    lane = lax.broadcasted_iota(jnp.int32, (WK, 128), 1)

    def b_one(k, acc):
        part = jnp.zeros((WK, 128), F32)
        for c in range(PD // LC):
            lanes = slice(c * LC, (c + 1) * LC)
            f = (x[k, :, lanes].astype(F32) - pe1[pl.ds(k, 1), lanes]) * wfull[w, :, lanes]
            for t in range(LC // 128):
                part = part + f[:, t * 128:(t + 1) * 128]
        return acc + jnp.where(lane == k, jnp.sum(part, axis=1, keepdims=True), 0.0)

    wt_col = jnp.sum(wfull[w], axis=1, keepdims=True)
    bt = lax.fori_loop(0, K, b_one, jnp.where(lane == K, wt_col, 0.0))
    b_pack[...] = bt[:32] + pltpu.roll(bt[32:], 64, 1)

    def b_copy(d):
        return to_prod(b_pack, b_recv.at[d], b_s.at[d], b_r.at[d], prod_peer(d))

    loop(1, NP, lambda d: b_copy(d).start())

    for d in (1, 3, 2):
        wx_arrived(d).wait_recv()
        wc_copy(d).start()
    for d in (0, 1, 3, 2):
        wc_arrived(d).wait_recv()

    def to_bf16(i):
        wb[pl.ds(pl.multiple_of(i * WK, WK), WK), :] = wfull[i].astype(BF16)

    loop(0, NW, to_bf16)
    hi, mid, lo = split3(wfull[w] / pt[...])
    rows = jnp.concatenate([hi, mid, lo], axis=0)
    m3 = lax.dot_general(rows, wb[...], NT, preferred_element_type=F32)
    m_own = m3[:WK] + (m3[WK:2 * WK] + m3[2 * WK:])
    for q in range(NP):
        m_stage[q] = m_own[(q // 4) * 8:(q // 4) * 8 + 8, (q % 4) * 128:(q % 4 + 1) * 128]

    def ms_copy(d):
        q = prod_peer(d)
        return to_prod(m_stage.at[q], m_recv.at[d], ms_s.at[d], ms_r.at[d], q)

    loop(1, NP, lambda d: ms_copy(d).start())

    loop(1, NP, lambda d: b_copy(d).wait_recv())
    packed = lax.fori_loop(1, NP, lambda d, a: a + b_recv[d], b_pack[...])
    own_rows = pl.ds(pl.multiple_of(w * WK, WK), WK)
    b_all[own_rows, :] = jnp.concatenate([packed, pltpu.roll(packed, 64, 1)], axis=0)

    def ba_copy(d):
        return to_week(b_all.at[own_rows], b_all.at[own_rows], ba_s.at[d], ba_r.at[d], week_peer(d))

    def ba_arrived(d):
        other = pl.ds(pl.multiple_of(lax.rem(w + NW - d, NW) * WK, WK), WK)
        return to_week(b_all.at[own_rows], b_all.at[other], ba_s.at[d], ba_r.at[d], week_peer(d))

    loop(1, NW, lambda d: ba_copy(d).start())

    b_own = b_all[own_rows, :]
    wt_own = jnp.sum(jnp.where(lane == K, b_own, 0.0), axis=1, keepdims=True)
    we_buf[pl.ds(0, WK), :] = b_own / wt_own

    def r_pair(j):
        we1 = we_buf[pl.ds(0, WK), :]
        cols = [
            jnp.sum(jnp.where(lane == 2 * j + e, we1, 0.0), axis=1, keepdims=True)
            for e in range(2)
        ]
        at = pl.ds(pl.multiple_of(j * 16, 16), 16)
        for c in range(PD // 256):
            lanes = slice(c * 256, (c + 1) * 256)
            cellw = wfull[w, :, lanes]
            fs = []
            for e in range(2):
                k = 2 * j + e
                f = x[k, :, lanes].astype(F32) - pe1[pl.ds(k, 1), lanes] - cols[e]
                fs.append(jnp.where(cellw > 0.0, f, 0.0))
            for g in range(8):
                s = slice(g * 8, g * 8 + 8)
                pair = jnp.concatenate([fs[0][s], fs[1][s]], axis=0)
                wpair = jnp.concatenate([fs[0][s] * cellw[s], fs[1][s] * cellw[s]], axis=0)
                q_buf[g, at, lanes] = pair.astype(BF16)
                u_buf[g, at, lanes] = wpair.astype(BF16)

    loop(0, K // 2, r_pair)

    def r_dot(g, acc):
        return acc + lax.dot_general(u_buf[g], q_buf[g], NT, preferred_element_type=F32)

    big = lax.fori_loop(0, 8, r_dot, jnp.zeros((K * 8, K * 8), F32))
    ri = lax.broadcasted_iota(jnp.int32, (K * 8, K * 8), 0)
    ci = lax.broadcasted_iota(jnp.int32, (K * 8, K * 8), 1)
    big = jnp.where(lax.rem(ri, 8) == lax.rem(ci, 8), big, 0.0)
    ei = lax.broadcasted_iota(jnp.int32, (K, K * 8), 0)
    ej = lax.broadcasted_iota(jnp.int32, (K, K * 8), 1)
    fold = jnp.where(ei == ej // 8, 1.0, 0.0)
    fi = lax.broadcasted_iota(jnp.int32, (K * 8, 128), 0)
    fj = lax.broadcasted_iota(jnp.int32, (K * 8, 128), 1)
    fold_t = jnp.where(fi // 8 == fj, 1.0, 0.0)
    half_done = lax.dot_general(fold, big, NN, precision=HI, preferred_element_type=F32)
    r2 = lax.dot_general(half_done, fold_t, NN, precision=HI, preferred_element_type=F32)
    r_pack[0] = r2[0:8] + pltpu.roll(r2[8:16], 32, 1) + pltpu.roll(r2[16:24], 64, 1) + pltpu.roll(r2[24:32], 96, 1)

    def rw_copy(d):
        return to_week(r_pack.at[0], r_week.at[d], rw_s.at[d], rw_r.at[d], week_peer(d))

    loop(1, NW, lambda d: rw_copy(d).start())

    loop(1, NP, lambda d: ms_copy(d).wait_recv())
    tile = lax.fori_loop(1, NP, lambda d, a: a + m_recv[d], m_stage[p])

    def tile_of(wk, q):
        return mm.at[
            pl.ds(pl.multiple_of(wk * WK + (q // 4) * 8, 8), 8),
            pl.ds(pl.multiple_of(lax.rem(q, 4) * 128, 128), 128),
        ]

    tile_of(w, p)[...] = tile

    def ma_copy(d):
        return to_prod(tile_of(w, p), tile_of(w, p), ma_s.at[d], ma_r.at[d], prod_peer(d))

    def ma_arrived(d):
        return to_prod(tile_of(w, p), tile_of(w, lax.rem(p + NP - d, NP)), ma_s.at[d], ma_r.at[d], prod_peer(d))

    loop(1, NP, lambda d: ma_copy(d).start())

    loop(1, NW, lambda d: rw_copy(d).wait_recv())
    r_sum = r_pack[0]
    for d in range(1, NW):
        r_sum = r_sum + r_week[d]
    r_pack[1] = r_sum

    def rp_copy(d):
        return to_prod(r_pack.at[1], r_prod.at[d], rp_s.at[d], rp_r.at[d], prod_peer(d))

    loop(1, NP, lambda d: rp_copy(d).start())

    loop(1, NP, lambda d: ma_arrived(d).wait_recv())

    def rows_of(wk):
        return mm.at[pl.ds(pl.multiple_of(wk * WK, WK), WK)]

    def mx_copy(d):
        return to_week(rows_of(w), rows_of(w), mx_s.at[d], mx_r.at[d], x_peer(d))

    def mx_arrived(d):
        return to_week(rows_of(w), rows_of(x_from(d)), mx_s.at[d], mx_r.at[d], x_peer(d))

    def mc_copy(d):
        slot = x_from(d)
        return to_week(rows_of(slot), rows_of(slot), mc_s.at[d], mc_r.at[d], sib)

    def mc_arrived(d):
        slot = x_from(d) + 1 - 2 * core
        return to_week(rows_of(slot), rows_of(slot), mc_s.at[d], mc_r.at[d], sib)

    for d in (1, 3, 2):
        mx_copy(d).start()
    mc_copy(0).start()

    loop(1, NW, lambda d: ba_arrived(d).wait_recv())
    loop(1, NP, lambda d: rp_copy(d).wait_recv())
    r_total = lax.fori_loop(1, NP, lambda d, a: a + r_prod[d], r_pack[1])
    b = b_all[...]
    lane_all = lax.broadcasted_iota(jnp.int32, (WEEKS, 128), 1)
    wt = jnp.sum(jnp.where(lane_all == K, b, 0.0), axis=1, keepdims=True)
    b = jnp.where(lane_all < K, b, 0.0)
    we1 = b / wt
    weight_total = jnp.sum(wt, axis=0, keepdims=True)

    for d in (1, 3, 2):
        mx_arrived(d).wait_recv()
        mc_copy(d).start()
    for d in (0, 1, 3, 2):
        mc_arrived(d).wait_recv()

    def apply_m(v):
        return lax.dot_general(mm[...], v, NN, precision=HI, preferred_element_type=F32)

    n1 = apply_m(we1)
    we2 = (b + n1) / wt
    we3 = (b + apply_m(we2)) / wt
    n3 = apply_m(we3)
    we4 = (b + n3) / wt
    we_buf[...] = we4
    we4_out[...] = we_buf[own_rows, :]

    we3_t = we3.T[:K]
    hi, mid, lo = split3(we3_t)
    rows = jnp.concatenate([hi, mid, lo], axis=0)
    wp3 = lax.dot_general(rows, wb[...], NN, preferred_element_type=F32)
    wp = wp3[:K] + (wp3[K:2 * K] + wp3[2 * K:])
    pe4_out[...] = pe1[...] - wp / pt[...]

    gram = lax.dot_general((we3 - we4).T[:K], n3, NN, precision=HI, preferred_element_type=F32)
    gram = gram - lax.dot_general(we3_t, n1, NN, precision=HI, preferred_element_type=F32)
    r_rows = jnp.concatenate(
        [r_total] + [pltpu.roll(r_total, 128 - 32 * a, 1) for a in range(1, 4)], axis=0
    )
    gram_out[...] = ((r_rows + gram) / weight_total)[:, :K]

    def drain_week(d):
        pt_copy(d).wait_send()
        ps_copy(d).wait_send()
        pe_copy(d).wait_send()
        ba_copy(d).wait_send()
        rw_copy(d).wait_send()

    loop(1, NW, drain_week)

    def drain_prod(d):
        b_copy(d).wait_send()
        ms_copy(d).wait_send()
        ma_copy(d).wait_send()
        rp_copy(d).wait_send()

    loop(1, NP, drain_prod)
    for d in range(NX):
        if d:
            wx_copy(d).wait_send()
            mx_copy(d).wait_send()
        wc_copy(d).wait_send()
        mc_copy(d).wait_send()


def effects(x, weights, first, last):
    vmem = pl.BlockSpec(memory_space=pltpu.VMEM)
    dma = pltpu.SemaphoreType.DMA
    scratch = [
        pltpu.VMEM((K, WK, PD), BF16),
        pltpu.VMEM((NW, WK, PD), F32),
        pltpu.VMEM((WEEKS, PD), BF16),
        pltpu.VMEM((NW, 1, PD), F32),
        pltpu.VMEM((1, PD), F32),
        pltpu.VMEM((NW, 8, HALF), F32),
        pltpu.VMEM((NW, 8, HALF), F32),
        pltpu.VMEM((NW, 8, HALF), F32),
        pltpu.VMEM((K, PD), F32),
        pltpu.VMEM((32, 128), F32),
        pltpu.VMEM((NP, 32, 128), F32),
        pltpu.VMEM((WEEKS, 128), F32),
        pltpu.VMEM((NP, 8, 128), F32),
        pltpu.VMEM((NP, 8, 128), F32),
        pltpu.VMEM((WEEKS, WEEKS), F32),
        pltpu.VMEM((8, K * 8, PD), BF16),
        pltpu.VMEM((8, K * 8, PD), BF16),
        pltpu.VMEM((2, 8, 128), F32),
        pltpu.VMEM((NW, 8, 128), F32),
        pltpu.VMEM((NP, 8, 128), F32),
        pltpu.VMEM((WEEKS, 128), F32),
        dma((4,)),
    ]
    for n in (NW, NW, NW, NX, NX, NP, NW, NP, NP, NX, NX, NW, NP):
        scratch += [dma((n,)), dma((n,))]
    return pl.pallas_call(
        effects_kernel,
        out_shape=(
            jax.ShapeDtypeStruct((K, PD), F32),
            jax.ShapeDtypeStruct((WK, 128), F32),
            jax.ShapeDtypeStruct((K, K), F32),
        ),
        in_specs=[pl.BlockSpec(memory_space=pl.ANY), vmem, vmem, vmem],
        out_specs=(vmem, vmem, vmem),
        scratch_shapes=scratch,
        compiler_params=pltpu.CompilerParams(
            collective_id=0, has_side_effects=True, vmem_limit_bytes=48 * 2**20
        ),
        name="effects",
    )(x, weights, first, last)


def per_device(regressors, weights, first_week, last_week):
    first = first_week.reshape(1, PD)
    last = last_week.reshape(1, PD)
    pe4, we4, gram = effects(regressors, weights, first, last)
    ids = lax.axis_index("week") * WK + lax.broadcasted_iota(jnp.int32, (WK, PD), 0)
    live = (ids >= first) & (ids <= last)
    field = regressors.astype(F32) - pe4[:, None, :] - we4[:, :K].T[:, :, None]
    return jnp.where(live[None], field, 0.0).astype(BF16), gram


def solution(mesh):
    return jax.shard_map(
        per_device,
        mesh=mesh,
        in_specs=(P(None, "week", "prod"), P("week", "prod"), P("prod"), P("prod")),
        out_specs=(P(None, "week", "prod"), P()),
        check_vma=False,
    )
```

time: 990 us -> 99.4 us (0.10)
  blocking collectives: 579 us -> 0 us
  waiting for transfers between devices: 302 us -> 0 us
  Pallas kernels: 0 us -> 87.1 us
  other arithmetic: 70.5 us -> 8.23 us
  matrix products: 24 us -> 0 us
  between operations: 13.8 us -> 0.67 us
    psum x6 -> x0, blocking collectives: 579 us -> none  [the longest x4 463 us: week_means(): return lax.psum(numer, 'prod') / week_total[None, :]]
    psum x4 -> x0, waiting for transfers between devices: 302 us -> none  [product_means(): return lax.psum(numer, 'week') / product_total[None, :]]
    pallas_call x0 -> x1, Pallas kernels: none -> 87.1 us  [effects(): pl.pallas_call(effects_kernel, out_shape=(jax.ShapeDtypeStruct((K, PD), F...]
    reduce_sum x9 -> x0, other arithmetic: 51.2 us -> none  [the longest x4 26.6 us: per_device(): jnp.sum(field * cell_weight[None], axis=1)]
    dot_general x1 -> x0, matrix products: 24 us -> none  [per_device(): jnp.einsum('kwp,lwp->kl', weighted, demeaned, precision=lax.Precision.HIG...]
    mul x1 -> x0, other arithmetic: 14 us -> none  [per_device(): weighted = demeaned * cell_weight[None]]
  transfers between devices with their start and end apart: 4 -> 0, of which waited for: 4 -> 0; matrix products, arithmetic and copies ran while one was open for 0% -> 0% of each run, Pallas kernels for 0% -> 0%
where the time goes in v1:
time: 99.4 us; the launch traced here: 99.1 us
  Pallas kernels  87.1 us (88%)
  other arithmetic  8.23 us (8%)
  local copies, waits for them, and re-layouts  3.07 us (3%)
    pallas_call x1, Pallas kernels, effects(): pl.pallas_call(effects_kernel, out_shape=(jax.ShapeDtypeStruct((K, PD), F...  87.1 us
    convert_element_type x1, other arithmetic, per_device(): return (jnp.where(live[None], field, 0.0).astype(BF16), gram)  7.37 us

profile of v1, /device:TPU:1, one launch (start us, length us, event | category | flops | bytes accessed | tf_op | source)
XLA Modules:
  0.0 99.1 jit_solution(2155279299931173447)
XLA Ops:
  0.6 0.7 reshape.63.first
  1.3 0.7 reshape.64.last
  2.0 0.9 compare_and_fusion
  2.9 0.0 copy-start
  2.9 1.0 copy-done
  3.9 87.1 %effects.1 = (f32[32,1536]{1,0:T(8,128)S(1)}, f32[64,128]{1,0:T(8,128)S(1)}, f32[32,32]{1,0:T(8,128)S(1)}) custom-call(bf16[32,64,1536]{2,1,0:T(8,128)(2,1)} %x_hbm.1, s32[64,1536]{1,0:T(8,128)S(1)} %copy-done, s32[1,1536]{1,0:T(1,128)S(1)} %reshape.63.first, s32[1,1536]{1,0:T(1,128)S(1)} %reshape.64.last), custom_call_target="tpu_custom_call" | custom-call | tf_op jit(solution)/shard_map/effects/pallas_call | solution.py:438
  91.1 0.1 copy.6
  91.1 7.4 %select_convert_fusion = bf16[32,64,1536]{2,1,0:T(8,128)(2,1)} fusion(bf16[32,64,1536]{2,1,0:T(8,128)(2,1)} %x_hbm.1, f32[32,64]{1,0:T(8,128)S(1)} %copy.6, f32[32,1536]{1,0:T(8,128)S(1)} %get-tuple-element.5, pred[64,1536]{1,0:T(8,128)(4,1)S(1)} %compare_and_fusion), kind=kLoop, calls=%fused_computation | loop fusion | flops 15728640 | bytes 12886016 | tf_op jit(solution)/shard_map/convert_element_type | solution.py:462
  98.5 0.6 copy.8
  (2 shorter events, 0.0 us)
Async XLA Ops:
  2.9 1.0 %copy-start = (s32[64,1536]{1,0:T(8,128)S(1)}, s32[64,1536]{1,0:T(8,128)}, u32[]{:S(2)}) copy-start(s32[64,1536]{1,0:T(8,128)} %weights.1) | copy-start | bytes 1179652

commit v2 on v1

v2 whole, which is shorter than its diff:
```python
import functools

import jax
import jax.numpy as jnp
from jax import lax
from jax.experimental import pallas as pl
from jax.experimental.pallas import tpu as pltpu
from jax.sharding import PartitionSpec as P

MESH = pl.DeviceIdType.MESH
F32 = jnp.float32
BF16 = jnp.bfloat16
HI = lax.Precision.HIGHEST
NT = (((1,), (1,)), ((), ()))
NN = (((1,), (0,)), ((), ()))

K = 32
WK = 64
PD = 1536
NW = 8
NX = 4
NP = 32
WEEKS = NW * WK
LC = 384
HALF = PD // 2
W_PARTS = (0, 16, 40, 64)


def split3(v):
    hi = v.astype(BF16)
    r = v - hi.astype(F32)
    mid = r.astype(BF16)
    lo = (r - mid.astype(F32)).astype(BF16)
    return hi, mid, lo


def loop(lo, hi, body):
    def step(i, carry):
        body(i)
        return carry

    lax.fori_loop(lo, hi, step, 0)


class Transfer:
    def __init__(self, ds, send, arrival=None):
        self.ds, self.send, self.arrival = ds, send, arrival or send
        self.sent, self.got = [], []

    def each(self, ds, act):
        if isinstance(ds, range) and len(ds) > 3:
            loop(ds.start, ds.stop, act)
        else:
            for d in ds:
                act(d)

    def start(self, ds=None):
        ds = self.ds if ds is None else ds
        self.each(ds, lambda d: self.send(d).start())
        self.sent += list(ds)

    def wait(self, ds=None):
        ds = self.ds if ds is None else ds
        self.each(ds, lambda d: self.arrival(d).wait_recv())
        self.got += list(ds)

    def drain(self):
        self.each(self.ds if len(self.sent) == len(self.ds) else self.sent, lambda d: self.send(d).wait_send())


def effects_kernel(
    x_hbm, weights_hbm, first_hbm, last_hbm,
    pe4_out, we4_out, gram_out,
    x, weights, first, last, wfull, wb, pt_own, pt_sib, pt_all, pt, wt_part, ps_stage, ps_sib, ps_recv, pe1_chunks, pe1,
    b_pack, b_recv, b_all, m_stage, m_recv, mm, m_hi, m_mid, m_lo,
    q_buf, u_buf, r_pack, r_week, r_prod, we_buf,
    x_sem, pt_s, pt_r, ps_s, ps_r, wt_s, wt_r, pe_s, pe_r, pf_s, pf_r, wx_s, wx_r, wc_s, wc_r, wy_s, wy_r, wd_s, wd_r,
    b_s, b_r, ba_s, ba_r, ms_s, ms_r, ma_s, ma_r, mx_s, mx_r, mc_s, mc_r,
    rw_s, rw_r, rp_s, rp_r,
):
    w = lax.axis_index("week")
    p = lax.axis_index("prod")
    xi = w // 2
    core = lax.rem(w, 2)
    sib = xi * 2 + (1 - core)

    def week_peer(d):
        return lax.rem(w + d, NW)

    def prod_peer(d):
        return lax.rem(p + d, NP)

    def x_peer(d):
        return lax.rem(xi + d, NX) * 2 + core

    def x_from(d):
        return lax.rem(xi + NX - d, NX) * 2 + core

    def to_week(src, dst, ssem, rsem, q):
        return pltpu.make_async_remote_copy(
            src_ref=src, dst_ref=dst, send_sem=ssem, recv_sem=rsem,
            device_id={"week": q}, device_id_type=MESH,
        )

    def to_prod(src, dst, ssem, rsem, q):
        return pltpu.make_async_remote_copy(
            src_ref=src, dst_ref=dst, send_sem=ssem, recv_sem=rsem,
            device_id={"prod": q}, device_id_type=MESH,
        )

    def x_copy(c):
        rows = pl.ds(c * 8, 8)
        return pltpu.make_async_copy(x_hbm.at[rows], x.at[rows], x_sem.at[c])

    weights_copy = pltpu.make_async_copy(weights_hbm, weights, x_sem.at[4])
    weights_copy.start()
    first_copy = pltpu.make_async_copy(first_hbm, first, x_sem.at[5])
    first_copy.start()
    last_copy = pltpu.make_async_copy(last_hbm, last, x_sem.at[6])
    last_copy.start()
    for c in range(4):
        x_copy(c).start()

    barrier = pltpu.get_barrier_semaphore()

    def greet_week(d):
        pl.semaphore_signal(barrier, inc=1, device_id={"week": week_peer(d)}, device_id_type=MESH)

    def greet_prod(d):
        pl.semaphore_signal(barrier, inc=1, device_id={"prod": prod_peer(d)}, device_id_type=MESH)

    loop(1, NW, greet_week)
    loop(1, NP, greet_prod)

    weights_copy.wait()
    first_copy.wait()
    last_copy.wait()
    ids = w * WK + lax.broadcasted_iota(jnp.int32, (WK, PD), 0)
    live = (ids >= first[...].reshape(1, PD)) & (ids <= last[...].reshape(1, PD))
    cell = jnp.where(live, weights[...].astype(F32), 0.0)
    wfull[w] = cell
    wb[pl.ds(pl.multiple_of(w * WK, WK), WK), :] = cell.astype(BF16)
    pt_own[...] = jnp.sum(cell, axis=0, keepdims=True)
    lane = lax.broadcasted_iota(jnp.int32, (WK, 128), 1)
    row = lax.broadcasted_iota(jnp.int32, (WK, 128), 0)
    wt_col = jnp.sum(cell, axis=1, keepdims=True)
    wt_part[p] = jnp.sum(jnp.where(lane == row, wt_col, 0.0), axis=0, keepdims=True)

    def sums_group(g, acc):
        x_copy(g).wait()

        def one(j, acc):
            k = g * 8 + j
            part = jnp.zeros((WK, 128), F32)
            for c in range(PD // LC):
                lanes = slice(c * LC, (c + 1) * LC)
                weighted = x[k, :, lanes].astype(F32) * wfull[w, :, lanes]
                half, off = c // 2, (c % 2) * LC
                ps_stage[half, g, pl.ds(j, 1), off:off + LC] = jnp.sum(weighted, axis=0, keepdims=True)
                for t in range(LC // 128):
                    part = part + weighted[:, t * 128:(t + 1) * 128]
            return acc + jnp.where(lane == k, jnp.sum(part, axis=1, keepdims=True), 0.0)

        return lax.fori_loop(0, 8, one, acc, unroll=2)

    ws = lax.fori_loop(0, 4, sums_group, jnp.zeros((WK, 128), F32))

    pl.semaphore_wait(barrier, NW - 1 + NP - 1)

    def pt_copy(d):
        if d == 0:
            return to_week(pt_own, pt_sib, pt_s.at[0], pt_r.at[0], sib)
        return to_week(pt_all.at[xi], pt_all.at[xi], pt_s.at[d], pt_r.at[d], x_peer(d))

    def pt_arrived(d):
        if d == 0:
            return pt_copy(0)
        return to_week(pt_all.at[xi], pt_all.at[lax.rem(xi + NX - d, NX)], pt_s.at[d], pt_r.at[d], x_peer(d))

    def ps_copy(d):
        if d == 0:
            return to_week(ps_stage.at[1 - core], ps_sib, ps_s.at[0], ps_r.at[0], sib)
        q = x_peer(d)
        return to_week(ps_stage.at[core, lax.rem(xi + d, NX)], ps_recv.at[d], ps_s.at[d], ps_r.at[d], q)

    pt_move = Transfer((0, 2, 1, 3), pt_copy, pt_arrived)
    ps_move = Transfer((0, 2, 1, 3), ps_copy)
    pt_move.start((0,))
    ps_move.start((0,))

    def wt_copy(d):
        return to_prod(wt_part.at[p], wt_part.at[p], wt_s.at[d], wt_r.at[d], prod_peer(d))

    def wt_arrived(d):
        return to_prod(wt_part.at[p], wt_part.at[lax.rem(p + NP - d, NP)], wt_s.at[d], wt_r.at[d], prod_peer(d))

    def first_half(chip, other):
        return jnp.where(chip < other, 0, 1)

    def half_of(slot, h):
        return wfull.at[slot, :, pl.ds(pl.multiple_of(h * HALF, HALF), HALF)]

    def chip_to(d):
        return lax.rem(xi + d, NX)

    def chip_from(d):
        return lax.rem(xi + NX - d, NX)

    def part_of(slot, h, e):
        lo, hi = W_PARTS[e], W_PARTS[e + 1]
        return wfull.at[slot, pl.ds(lo, hi - lo), pl.ds(pl.multiple_of(h * HALF, HALF), HALF)]

    def wx_copy(i):
        d, e = i % NX, i // NX
        h = first_half(chip_to(d), xi)
        return to_week(part_of(w, h, e), part_of(w, h, e), wx_s.at[i], wx_r.at[i], x_peer(d))

    def wx_arrived(i):
        d, e = i % NX, i // NX
        h = first_half(xi, chip_from(d))
        return to_week(part_of(w, h, e), part_of(x_from(d), h, e), wx_s.at[i], wx_r.at[i], x_peer(d))

    def wy_copy(d):
        h = 1 - first_half(chip_to(d), xi)
        return to_week(half_of(w, h), half_of(w, h), wy_s.at[d], wy_r.at[d], x_peer(d))

    def wy_arrived(d):
        h = 1 - first_half(xi, chip_from(d))
        return to_week(half_of(w, h), half_of(x_from(d), h), wy_s.at[d], wy_r.at[d], x_peer(d))

    def other_core(slot):
        return slot + 1 - 2 * core

    def wc_copy(i):
        d, e = i % NX, i // NX
        if d == 0:
            return to_week(wfull.at[w], wfull.at[w], wc_s.at[i], wc_r.at[i], sib)
        here = part_of(x_from(d), first_half(xi, chip_from(d)), e)
        return to_week(here, here, wc_s.at[i], wc_r.at[i], sib)

    def wc_arrived(i):
        d, e = i % NX, i // NX
        if d == 0:
            return to_week(wfull.at[w], wfull.at[sib], wc_s.at[i], wc_r.at[i], sib)
        here = part_of(other_core(x_from(d)), first_half(xi, chip_from(d)), e)
        return to_week(here, here, wc_s.at[i], wc_r.at[i], sib)

    def wd_copy(d):
        here = half_of(x_from(d), 1 - first_half(xi, chip_from(d)))
        return to_week(here, here, wd_s.at[d], wd_r.at[d], sib)

    def wd_arrived(d):
        here = half_of(other_core(x_from(d)), 1 - first_half(xi, chip_from(d)))
        return to_week(here, here, wd_s.at[d], wd_r.at[d], sib)

    wt_move = Transfer(range(1, NP), wt_copy, wt_arrived)
    wt_move.start()
    parts = range(len(W_PARTS) - 1)
    wx_move = Transfer([d + NX * e for e in parts for d in (2, 1, 3)], wx_copy, wx_arrived)
    wc_move = Transfer([0] + [d + NX * e for e in parts for d in (1, 3, 2)], wc_copy, wc_arrived)
    wy_move = Transfer((2, 1, 3), wy_copy, wy_arrived)
    wd_move = Transfer((1, 3, 2), wd_copy, wd_arrived)

    def send_part(e):
        wx_move.start([d + NX * e for d in (2, 1, 3)])

    send_part(0)
    pt_move.wait((0,))
    pt_all[xi] = pt_own[...] + pt_sib[...]
    ps_move.wait((0,))
    for a in range(NX):
        ps_stage[core, a] = ps_stage[core, a] + ps_sib[a]
    pt_move.start((2, 1, 3))
    ps_move.start((2, 1, 3))
    wc_move.start((0,))
    send_part(1)
    pt_move.wait((2, 1, 3))
    ps_move.wait((2, 1, 3))
    pt[...] = jnp.sum(pt_all[...], axis=0)
    total = ps_stage[core, xi]
    for d in range(1, NX):
        total = total + ps_recv[d]
    own_half = pl.ds(pl.multiple_of(core * HALF, HALF), HALF)
    pe1_chunks[w] = total / pt[:, own_half]

    def pe_copy(d):
        return to_week(pe1_chunks.at[w], pe1_chunks.at[w], pe_s.at[d], pe_r.at[d], x_peer(d))

    def pe_arrived(d):
        return to_week(pe1_chunks.at[w], pe1_chunks.at[x_from(d)], pe_s.at[d], pe_r.at[d], x_peer(d))

    def pf_copy(d):
        slot = x_from(d)
        return to_week(pe1_chunks.at[slot], pe1_chunks.at[slot], pf_s.at[d], pf_r.at[d], sib)

    def pf_arrived(d):
        slot = other_core(x_from(d))
        return to_week(pe1_chunks.at[slot], pe1_chunks.at[slot], pf_s.at[d], pf_r.at[d], sib)

    pe_move = Transfer((2, 1, 3), pe_copy, pe_arrived)
    pf_move = Transfer((0, 1, 3, 2), pf_copy, pf_arrived)
    pe_move.start()
    pf_move.start((0,))
    for e in parts[2:]:
        send_part(e)

    def wb_half(slot, h):
        return wb.at[
            pl.ds(pl.multiple_of(slot * WK, WK), WK),
            pl.ds(pl.multiple_of(h * HALF, HALF), HALF),
        ]

    for e in parts[:2]:
        for d in (1, 3, 2):
            wx_move.wait((d + NX * e,))
            wc_move.start((d + NX * e,))

    for d in (1, 3, 2):
        pe_move.wait((d,))
        pf_move.start((d,))
    pf_move.wait()
    for r in range(NW):
        pe1[(r // 2) * 8:(r // 2) * 8 + 8, (r % 2) * HALF:(r % 2 + 1) * HALF] = pe1_chunks[r]
    hi, mid, lo = split3(pe1[...])
    pe_rows = jnp.concatenate([hi, mid, lo, jnp.zeros((K, PD), BF16)], axis=0)
    own_wb = wb[pl.ds(pl.multiple_of(w * WK, WK), WK), :]
    taken = lax.dot_general(own_wb, pe_rows, NT, preferred_element_type=F32)
    taken = taken + (pltpu.roll(taken, 128 - K, 1) + pltpu.roll(taken, 128 - 2 * K, 1))
    bt = jnp.where(lane < K, ws - taken, 0.0)
    b_pack[...] = sum(
        [pltpu.roll(bt[16 * a:16 * a + 16], 32 * a, 1) for a in range(1, 4)], bt[:16]
    )

    def b_copy(d):
        return to_prod(b_pack, b_recv.at[d], b_s.at[d], b_r.at[d], prod_peer(d))

    b_move = Transfer(range(1, NP), b_copy)
    b_move.start()

    for e in parts[2:]:
        for d in (1, 3, 2):
            wx_move.wait((d + NX * e,))
            wc_move.start((d + NX * e,))
    hi, mid, lo = split3(wfull[w] / pt[...])
    wc_move.wait()

    for h in (0, 1):
        wb_half(sib, h)[...] = half_of(sib, h)[...].astype(BF16)

    def to_bf16(i):
        d = 1 + i // 2
        slot = chip_from(d) * 2 + lax.rem(i, 2)
        h = first_half(xi, chip_from(d))
        wb_half(slot, h)[...] = half_of(slot, h)[...].astype(BF16)
        wb_half(slot, 1 - h)[...] = jnp.zeros((WK, HALF), BF16)

    loop(0, NW - 2, to_bf16)
    rows = jnp.concatenate([hi, mid, lo], axis=0)
    m3 = lax.dot_general(rows, wb[...], NT, preferred_element_type=F32)
    m_own = m3[:WK] + (m3[WK:2 * WK] + m3[2 * WK:])
    for q in range(NP):
        m_stage[q] = m_own[(q // 4) * 8:(q // 4) * 8 + 8, (q % 4) * 128:(q % 4 + 1) * 128]

    def ms_copy(d):
        q = prod_peer(d)
        return to_prod(m_stage.at[q], m_recv.at[d], ms_s.at[d], ms_r.at[d], q)

    ms_move = Transfer(range(1, NP), ms_copy)
    ms_move.start()
    wy_move.start()

    b_move.wait()
    wt_move.wait()
    wt_row = lax.fori_loop(0, NP, lambda d, a: a + wt_part[d], jnp.zeros((1, 128), F32))
    wt_own = jnp.sum(jnp.where(lane == row, wt_row, 0.0), axis=1, keepdims=True)
    packed = lax.fori_loop(1, NP, lambda d, a: a + b_recv[d], b_pack[...])
    b_own = jnp.concatenate(
        [packed] + [pltpu.roll(packed, 128 - 32 * a, 1) for a in range(1, 4)], axis=0
    )
    b_own = jnp.where(lane < K, b_own, jnp.where(lane == K, wt_own, 0.0))
    b_all[w] = b_own[:32] + pltpu.roll(b_own[32:], 64, 1)
    own_rows = pl.ds(pl.multiple_of(w * WK, WK), WK)

    def ba_copy(d):
        return to_week(b_all.at[w], b_all.at[w], ba_s.at[d], ba_r.at[d], week_peer(d))

    def ba_arrived(d):
        return to_week(b_all.at[w], b_all.at[lax.rem(w + NW - d, NW)], ba_s.at[d], ba_r.at[d], week_peer(d))

    ba_move = Transfer(range(1, NW), ba_copy, ba_arrived)
    ba_move.start()

    we_buf[pl.ds(0, WK), :] = b_own / wt_own

    def r_pair(j):
        we1 = we_buf[pl.ds(0, WK), :]
        cols = [
            jnp.sum(jnp.where(lane == 2 * j + e, we1, 0.0), axis=1, keepdims=True)
            for e in range(2)
        ]
        at = pl.ds(pl.multiple_of(j * 16, 16), 16)
        for c in range(PD // 256):
            lanes = slice(c * 256, (c + 1) * 256)
            cellw = wfull[w, :, lanes]
            fs = []
            for e in range(2):
                k = 2 * j + e
                f = x[k, :, lanes].astype(F32) - pe1[pl.ds(k, 1), lanes] - cols[e]
                fs.append(jnp.where(cellw > 0.0, f, 0.0))
            for g in range(8):
                s = slice(g * 8, g * 8 + 8)
                pair = jnp.concatenate([fs[0][s], fs[1][s]], axis=0)
                wpair = jnp.concatenate([fs[0][s] * cellw[s], fs[1][s] * cellw[s]], axis=0)
                q_buf[g, at, lanes] = pair.astype(BF16)
                u_buf[g, at, lanes] = wpair.astype(BF16)

    loop(0, K // 2, r_pair)

    ms_move.wait()
    tile = lax.fori_loop(1, NP, lambda d, a: a + m_recv[d], m_stage[p])

    def tile_of(wk, q):
        return mm.at[
            pl.ds(pl.multiple_of(wk * WK + (q // 4) * 8, 8), 8),
            pl.ds(pl.multiple_of(lax.rem(q, 4) * 128, 128), 128),
        ]

    tile_of(w, p)[...] = tile

    def ma_copy(d):
        return to_prod(tile_of(w, p), tile_of(w, p), ma_s.at[d], ma_r.at[d], prod_peer(d))

    def ma_arrived(d):
        return to_prod(tile_of(w, p), tile_of(w, lax.rem(p + NP - d, NP)), ma_s.at[d], ma_r.at[d], prod_peer(d))

    ma_move = Transfer(range(1, NP), ma_copy, ma_arrived)
    ma_move.start()

    def r_dot(g, acc):
        return acc + lax.dot_general(u_buf[g], q_buf[g], NT, preferred_element_type=F32)

    big = lax.fori_loop(0, 8, r_dot, jnp.zeros((K * 8, K * 8), F32))
    ri = lax.broadcasted_iota(jnp.int32, (K * 8, K * 8), 0)
    ci = lax.broadcasted_iota(jnp.int32, (K * 8, K * 8), 1)
    big = jnp.where(lax.rem(ri, 8) == lax.rem(ci, 8), big, 0.0)
    ei = lax.broadcasted_iota(jnp.int32, (K, K * 8), 0)
    ej = lax.broadcasted_iota(jnp.int32, (K, K * 8), 1)
    fold = jnp.where(ei == ej // 8, 1.0, 0.0)
    fi = lax.broadcasted_iota(jnp.int32, (K * 8, 128), 0)
    fj = lax.broadcasted_iota(jnp.int32, (K * 8, 128), 1)
    fold_t = jnp.where(fi // 8 == fj, 1.0, 0.0)
    half_done = lax.dot_general(fold, big, NN, precision=HI, preferred_element_type=F32)
    r2 = lax.dot_general(half_done, fold_t, NN, precision=HI, preferred_element_type=F32)
    r_pack[0] = r2[0:8] + pltpu.roll(r2[8:16], 32, 1) + pltpu.roll(r2[16:24], 64, 1) + pltpu.roll(r2[24:32], 96, 1)

    def rw_copy(d):
        return to_week(r_pack.at[0], r_week.at[d], rw_s.at[d], rw_r.at[d], week_peer(d))

    rw_move = Transfer(range(1, NW), rw_copy)
    rw_move.start()

    ma_move.wait()

    def rows_of(wk):
        return mm.at[pl.ds(pl.multiple_of(wk * WK, WK), WK)]

    def mx_copy(d):
        return to_week(rows_of(w), rows_of(w), mx_s.at[d], mx_r.at[d], x_peer(d))

    def mx_arrived(d):
        return to_week(rows_of(w), rows_of(x_from(d)), mx_s.at[d], mx_r.at[d], x_peer(d))

    def mc_copy(d):
        slot = x_from(d)
        return to_week(rows_of(slot), rows_of(slot), mc_s.at[d], mc_r.at[d], sib)

    def mc_arrived(d):
        slot = x_from(d) + 1 - 2 * core
        return to_week(rows_of(slot), rows_of(slot), mc_s.at[d], mc_r.at[d], sib)

    mx_move = Transfer((1, 3, 2), mx_copy, mx_arrived)
    mc_move = Transfer((0, 1, 3, 2), mc_copy, mc_arrived)
    mx_move.start()
    mc_move.start((0,))

    rw_move.wait()
    r_sum = r_pack[0]
    for d in range(1, NW):
        r_sum = r_sum + r_week[d]
    r_pack[1] = r_sum

    def rp_copy(d):
        return to_prod(r_pack.at[1], r_prod.at[d], rp_s.at[d], rp_r.at[d], prod_peer(d))

    rp_move = Transfer(range(1, NP), rp_copy)
    rp_move.start()
    for d in (1, 3, 2):
        mx_move.wait((d,))
        mc_move.start((d,))
    for d in (1, 3, 2):
        wy_move.wait((d,))
        wd_move.start((d,))
    wd_move.wait()

    def rest_to_bf16(i):
        d = 1 + i // 2
        slot = chip_from(d) * 2 + lax.rem(i, 2)
        h = 1 - first_half(xi, chip_from(d))
        wb_half(slot, h)[...] = half_of(slot, h)[...].astype(BF16)

    loop(0, NW - 2, rest_to_bf16)

    ba_move.wait()
    lane_all = lax.broadcasted_iota(jnp.int32, (WEEKS, 128), 1)
    pieces = []
    for i in range(NW):
        piece = b_all[i]
        pieces += [piece, pltpu.roll(piece, 64, 1)]
    b = jnp.concatenate(pieces, axis=0)
    wt = jnp.sum(jnp.where(lane_all == K, b, 0.0), axis=1, keepdims=True)
    b = jnp.where(lane_all < K, b, 0.0)
    we1 = b / wt
    weight_total = jnp.sum(wt, axis=0, keepdims=True)

    mc_move.wait()

    def put_m(rows, cols, v):
        hi, mid, lo = split3(v)
        m_hi[rows, cols] = hi
        m_mid[rows, cols] = mid
        m_lo[rows, cols] = lo

    blocks = [slice(a * 128, a * 128 + 128) for a in range(NX)]
    for a in range(NX):
        put_m(blocks[a], blocks[a], mm[blocks[a], blocks[a]])
        for c in range(a + 1, NX):
            both = mm[blocks[a], blocks[c]] + mm[blocks[c], blocks[a]].T
            put_m(blocks[a], blocks[c], both)
            put_m(blocks[c], blocks[a], both.T)

    def apply_m(v):
        hi, mid, lo = [part.astype(F32) for part in split3(v)]
        parts = (hi + pltpu.roll(mid, K, 1) + pltpu.roll(lo, 2 * K, 1)).astype(BF16)
        acc = jnp.dot(m_hi[...], parts, preferred_element_type=F32)
        acc = acc + jnp.where(lane_all < 2 * K, jnp.dot(m_mid[...], parts, preferred_element_type=F32), 0.0)
        acc = acc + jnp.where(lane_all < K, jnp.dot(m_lo[...], parts, preferred_element_type=F32), 0.0)
        acc = acc + (pltpu.roll(acc, 128 - K, 1) + pltpu.roll(acc, 128 - 2 * K, 1))
        return jnp.where(lane_all < K, acc, 0.0)

    n1 = apply_m(we1)
    we2 = (b + n1) / wt
    we3 = (b + apply_m(we2)) / wt
    n3 = apply_m(we3)
    we4 = (b + n3) / wt
    we_buf[...] = we4
    we4_out[...] = we_buf[own_rows, :]

    we3_t = we3.T[:K]
    hi, mid, lo = split3(we3_t)
    rows = jnp.concatenate([hi, mid, lo], axis=0)
    wp3 = lax.dot_general(rows, wb[...], NN, preferred_element_type=F32)
    wp = wp3[:K] + (wp3[K:2 * K] + wp3[2 * K:])
    pe4_out[...] = pe1[...] - wp / pt[...]

    rp_move.wait()
    r_total = lax.fori_loop(1, NP, lambda d, a: a + r_prod[d], r_pack[1])
    gram = lax.dot_general((we3 - we4).T[:K], n3, NN, precision=HI, preferred_element_type=F32)
    gram = gram - lax.dot_general(we3_t, n1, NN, precision=HI, preferred_element_type=F32)
    r_rows = jnp.concatenate(
        [r_total] + [pltpu.roll(r_total, 128 - 32 * a, 1) for a in range(1, 4)], axis=0
    )
    gram_out[...] = ((r_rows + gram) / weight_total)[:, :K]

    for move in (
        pt_move, ps_move, wt_move, wx_move, wc_move, wy_move, wd_move, pe_move, pf_move, b_move, ba_move,
        ms_move, ma_move, mx_move, mc_move, rw_move, rp_move,
    ):
        move.drain()


def effects(x, weights, first, last):
    vmem = pl.BlockSpec(memory_space=pltpu.VMEM)
    dma = pltpu.SemaphoreType.DMA
    scratch = [
        pltpu.VMEM((K, WK, PD), BF16),
        pltpu.VMEM((WK, PD), jnp.int32),
        pltpu.VMEM((PD,), jnp.int32),
        pltpu.VMEM((PD,), jnp.int32),
        pltpu.VMEM((NW, WK, PD), F32),
        pltpu.VMEM((WEEKS, PD), BF16),
        pltpu.VMEM((1, PD), F32),
        pltpu.VMEM((1, PD), F32),
        pltpu.VMEM((NX, 1, PD), F32),
        pltpu.VMEM((1, PD), F32),
        pltpu.VMEM((NP, 1, 128), F32),
        pltpu.VMEM((2, NX, 8, HALF), F32),
        pltpu.VMEM((NX, 8, HALF), F32),
        pltpu.VMEM((NX, 8, HALF), F32),
        pltpu.VMEM((NW, 8, HALF), F32),
        pltpu.VMEM((K, PD), F32),
        pltpu.VMEM((16, 128), F32),
        pltpu.VMEM((NP, 16, 128), F32),
        pltpu.VMEM((NW, 32, 128), F32),
        pltpu.VMEM((NP, 8, 128), F32),
        pltpu.VMEM((NP, 8, 128), F32),
        pltpu.VMEM((WEEKS, WEEKS), F32),
        pltpu.VMEM((WEEKS, WEEKS), BF16),
        pltpu.VMEM((WEEKS, WEEKS), BF16),
        pltpu.VMEM((WEEKS, WEEKS), BF16),
        pltpu.VMEM((8, K * 8, PD), BF16),
        pltpu.VMEM((8, K * 8, PD), BF16),
        pltpu.VMEM((2, 8, 128), F32),
        pltpu.VMEM((NW, 8, 128), F32),
        pltpu.VMEM((NP, 8, 128), F32),
        pltpu.VMEM((WEEKS, 128), F32),
        dma((7,)),
    ]
    for n in (NX, NX, NP, NX, NX, len(W_PARTS) * NX, len(W_PARTS) * NX, NX, NX, NP, NW, NP, NP, NX, NX, NW, NP):
        scratch += [dma((n,)), dma((n,))]
    return pl.pallas_call(
        effects_kernel,
        out_shape=(
            jax.ShapeDtypeStruct((K, PD), F32),
            jax.ShapeDtypeStruct((WK, 128), F32),
            jax.ShapeDtypeStruct((K, K), F32),
        ),
        in_specs=[pl.BlockSpec(memory_space=pl.ANY)] * 4,
        out_specs=(vmem, vmem, vmem),
        scratch_shapes=scratch,
        compiler_params=pltpu.CompilerParams(
            collective_id=0, has_side_effects=True, vmem_limit_bytes=48 * 2**20
        ),
        name="effects",
    )(x, weights, first, last)


KB = 4


def output_kernel(x, first, last, pe4, we4, gram, out, gram_out):
    w = lax.axis_index("week")
    step = pl.program_id(0)
    gram_out[...] = gram[...]
    lane = lax.broadcasted_iota(jnp.int32, (WK, 128), 1)
    ids = w * WK + lax.broadcasted_iota(jnp.int32, (WK, LC), 0)
    cols = [
        jnp.sum(jnp.where(lane == step * KB + e, we4[...], 0.0), axis=1, keepdims=True)
        for e in range(KB)
    ]
    first_row = first[...].reshape(1, PD)
    last_row = last[...].reshape(1, PD)
    for c in range(PD // LC):
        lanes = slice(c * LC, (c + 1) * LC)
        live = (ids >= first_row[:, lanes]) & (ids <= last_row[:, lanes])
        for e in range(KB):
            field = x[e, :, lanes].astype(F32) - pe4[pl.ds(step * KB + e, 1), lanes] - cols[e]
            out[e, :, lanes] = jnp.where(live, field, 0.0).astype(BF16)


def output(x, first, last, pe4, we4, gram):
    vmem = pl.BlockSpec(memory_space=pltpu.VMEM)
    block = pl.BlockSpec((KB, WK, PD), lambda i: (i, 0, 0))
    return pl.pallas_call(
        output_kernel,
        grid=(K // KB,),
        out_shape=(
            jax.ShapeDtypeStruct((K, WK, PD), BF16),
            jax.ShapeDtypeStruct((K, K), F32),
        ),
        in_specs=[block, vmem, vmem, vmem, vmem, vmem],
        out_specs=(block, vmem),
        compiler_params=pltpu.CompilerParams(vmem_limit_bytes=32 * 2**20),
        name="output",
    )(x, first, last, pe4, we4, gram)


def per_device(regressors, weights, first_week, last_week):
    pe4, we4, gram = effects(regressors, weights, first_week, last_week)
    return output(regressors, first_week, last_week, pe4, we4, gram)


def solution(mesh):
    return jax.shard_map(
        per_device,
        mesh=mesh,
        in_specs=(P(None, "week", "prod"), P("week", "prod"), P("prod"), P("prod")),
        out_specs=(P(None, "week", "prod"), P()),
        check_vma=False,
    )
```

time: 99.4 us -> 74.6 us (0.75)
  Pallas kernels: 87.1 us -> 70.9 us
  other arithmetic: 8.23 us -> 0 us
    pallas_call x1, Pallas kernels: 87.1 us -> 65.7 us  [effects(): pl.pallas_call(effects_kernel, out_shape=(jax.ShapeDtypeStruct((K, PD), F...]
    convert_element_type x1 -> x0, other arithmetic: 7.37 us -> none  [per_device(): return (jnp.where(live[None], field, 0.0).astype(BF16), gram)]
    pallas_call x0 -> x1, Pallas kernels: none -> 5.26 us  [output(): pl.pallas_call(output_kernel, grid=(K // KB,), out_shape=(jax.ShapeDtypeS...]
    reshape x2 -> x0, local copies, waits for them, and re-layouts: 1.41 us -> none  [the longest x1 0.7 us: per_device(): first = first_week.reshape(1, PD)]
    unnamed x3 -> x8, local copies, waits for them, and re-layouts: 1.6 us -> 2.77 us
where the time goes in v2:
time: 74.6 us; the launch traced here: 74.4 us
  Pallas kernels  70.9 us (95%)
  local copies, waits for them, and re-layouts  2.77 us (4%)
    pallas_call x1, Pallas kernels, effects(): pl.pallas_call(effects_kernel, out_shape=(jax.ShapeDtypeStruct((K, PD), F...  65.7 us
    pallas_call x1, Pallas kernels, output(): pl.pallas_call(output_kernel, grid=(K // KB,), out_shape=(jax.ShapeDtypeS...  5.26 us
    unnamed x8, local copies, waits for them, and re-layouts  2.77 us

profile of v2, /device:TPU:1, one launch (start us, length us, event | category | flops | bytes accessed | tf_op | source)
XLA Modules:
  0.0 74.4 jit_solution(8589423889053401673)
XLA Ops:
  0.6 0.0 copy-start
  0.6 0.0 copy-start.1
  0.7 1.1 %copy-done.1 = s32[64,1536]{1,0:T(8,128)S(1)} copy-done((s32[64,1536]{1,0:T(8,128)S(1)}, s32[64,1536]{1,0:T(8,128)}, u32[]{:S(2)}) %copy-start.1) | copy-done | bytes 393240
  1.8 0.0 copy-start.2
  1.8 0.9 %copy-done.2 = s32[1536]{0:T(1024)S(1)} copy-done((s32[1536]{0:T(1024)S(1)}, s32[1536]{0:T(1024)}, u32[]{:S(2)}) %copy-start.2) | copy-done | bytes 6168
  2.7 0.0 copy-start.3
  2.7 0.7 copy-done.3
  3.4 65.7 %effects.1 = (f32[32,1536]{1,0:T(8,128)S(1)}, f32[64,128]{1,0:T(8,128)S(1)}, f32[32,32]{1,0:T(8,128)S(1)}) custom-call(bf16[32,64,1536]{2,1,0:T(8,128)(2,1)} %x.1, s32[64,1536]{1,0:T(8,128)S(1)} %copy-done.1, s32[1536]{0:T(1024)S(1)} %copy-done.2, s32[1536]{0:T(1024)S(1)} %copy-done.3), custom_call_target="tpu_custom_call" | custom-call | tf_op jit(solution)/shard_map/effects/pallas_call | solution.py:620
  69.1 0.0 copy-done
  69.1 5.3 %output.1 = (bf16[32,64,1536]{2,1,0:T(8,128)(2,1)}, f32[32,32]{1,0:T(8,128)}) custom-call(bf16[32,64,1536]{2,1,0:T(8,128)(2,1)S(1)} %copy-done, s32[1536]{0:T(1024)S(1)} %copy-done.2, s32[1536]{0:T(1024)S(1)} %copy-done.3, f32[32,1536]{1,0:T(8,128)S(1)} %get-tuple-element.5.pe4, f32[64,128]{1,0:T(8,128)S(1)} %get-tuple-element.6.we4, ...), custom_call_target="tpu_custom_call" | custom-call | tf_op jit(solution)/shard_map/output/pallas_call | solution.py:663
Async XLA Ops:
  0.6 68.5 %copy-start = (bf16[32,64,1536]{2,1,0:T(8,128)(2,1)S(1)}, bf16[32,64,1536]{2,1,0:T(8,128)(2,1)}, u32[]{:S(2)}) copy-start(bf16[32,64,1536]{2,1,0:T(8,128)(2,1)} %x.1) | copy-start | bytes 18874372
  0.6 1.1 %copy-start.1 = (s32[64,1536]{1,0:T(8,128)S(1)}, s32[64,1536]{1,0:T(8,128)}, u32[]{:S(2)}) copy-start(s32[64,1536]{1,0:T(8,128)} %weights_hbm.1) | copy-start | bytes 1179652
  1.8 0.9 %copy-start.2 = (s32[1536]{0:T(1024)S(1)}, s32[1536]{0:T(1024)}, u32[]{:S(2)}) copy-start(s32[1536]{0:T(1024)} %first.1) | copy-start | bytes 18436
  2.7 0.7 copy-start.3

commit v3 on v2

--- a/solution.py
+++ b/solution.py
@@ -24,6 +24,8 @@
 LC = 384
 HALF = PD // 2
 W_PARTS = (0, 16, 40, 64)
+R_FIRST = 8
+VMEM_LIMIT = 53 * 2**20
 
 
 def split3(v):
@@ -69,13 +71,13 @@
 
 
 def effects_kernel(
-    x_hbm, weights_hbm, first_hbm, last_hbm,
+    x_hbm, cell_in,
     pe4_out, we4_out, gram_out,
-    x, weights, first, last, wfull, wb, pt_own, pt_sib, pt_all, pt, wt_part, ps_stage, ps_sib, ps_recv, pe1_chunks, pe1,
-    b_pack, b_recv, b_all, m_stage, m_recv, mm, m_hi, m_mid, m_lo,
+    x, wfull, wb, pt_own, pt_sib, pt_all, pt, wt_part, ps_stage, ps_sib, ps_recv, pe1_chunks, pe1,
+    b_pack, b_y, b_z, b_all, m_stage, m_recv, mm, m_hi, m_mid, m_lo,
     q_buf, u_buf, r_pack, r_week, r_prod, we_buf,
     x_sem, pt_s, pt_r, ps_s, ps_r, wt_s, wt_r, pe_s, pe_r, pf_s, pf_r, wx_s, wx_r, wc_s, wc_r, wy_s, wy_r, wd_s, wd_r,
-    b_s, b_r, ba_s, ba_r, ms_s, ms_r, ma_s, ma_r, mx_s, mx_r, mc_s, mc_r,
+    by_s, by_r, bz_s, bz_r, ba_s, ba_r, ms_s, ms_r, ma_s, ma_r, mx_s, mx_r, mc_s, mc_r,
     rw_s, rw_r, rp_s, rp_r,
 ):
     w = lax.axis_index("week")
@@ -90,6 +92,11 @@
     def prod_peer(d):
         return lax.rem(p + d, NP)
 
+    def grid_peer(d, sign):
+        y = lax.rem(p // 8 + 4 + sign * (d // 8), 4)
+        z = lax.rem(lax.rem(p, 8) + 8 + sign * (d % 8), 8)
+        return y * 8 + z
+
     def x_peer(d):
         return lax.rem(xi + d, NX) * 2 + core
 
@@ -112,12 +119,6 @@
         rows = pl.ds(c * 8, 8)
         return pltpu.make_async_copy(x_hbm.at[rows], x.at[rows], x_sem.at[c])
 
-    weights_copy = pltpu.make_async_copy(weights_hbm, weights, x_sem.at[4])
-    weights_copy.start()
-    first_copy = pltpu.make_async_copy(first_hbm, first, x_sem.at[5])
-    first_copy.start()
-    last_copy = pltpu.make_async_copy(last_hbm, last, x_sem.at[6])
-    last_copy.start()
     for c in range(4):
         x_copy(c).start()
 
@@ -132,12 +133,7 @@
     loop(1, NW, greet_week)
     loop(1, NP, greet_prod)
 
-    weights_copy.wait()
-    first_copy.wait()
-    last_copy.wait()
-    ids = w * WK + lax.broadcasted_iota(jnp.int32, (WK, PD), 0)
-    live = (ids >= first[...].reshape(1, PD)) & (ids <= last[...].reshape(1, PD))
-    cell = jnp.where(live, weights[...].astype(F32), 0.0)
+    cell = cell_in[...]
     wfull[w] = cell
     wb[pl.ds(pl.multiple_of(w * WK, WK), WK), :] = cell.astype(BF16)
     pt_own[...] = jnp.sum(cell, axis=0, keepdims=True)
@@ -327,20 +323,28 @@
     taken = lax.dot_general(own_wb, pe_rows, NT, preferred_element_type=F32)
     taken = taken + (pltpu.roll(taken, 128 - K, 1) + pltpu.roll(taken, 128 - 2 * K, 1))
     bt = jnp.where(lane < K, ws - taken, 0.0)
-    b_pack[...] = sum(
+    b_pack[0] = sum(
         [pltpu.roll(bt[16 * a:16 * a + 16], 32 * a, 1) for a in range(1, 4)], bt[:16]
     )
 
-    def b_copy(d):
-        return to_prod(b_pack, b_recv.at[d], b_s.at[d], b_r.at[d], prod_peer(d))
-
-    b_move = Transfer(range(1, NP), b_copy)
-    b_move.start()
+    def by_copy(d):
+        return to_prod(b_pack.at[0], b_y.at[d], by_s.at[d], by_r.at[d], grid_peer(8 * d, 1))
+
+    def bz_copy(d):
+        return to_prod(b_pack.at[1], b_z.at[d], bz_s.at[d], bz_r.at[d], grid_peer(d, 1))
+
+    by_move = Transfer((2, 1, 3), by_copy)
+    bz_move = Transfer((4, 3, 5, 2, 6, 1, 7), bz_copy)
+    by_move.start()
 
     for e in parts[2:]:
         for d in (1, 3, 2):
             wx_move.wait((d + NX * e,))
             wc_move.start((d + NX * e,))
+    wy_move.start()
+    by_move.wait()
+    b_pack[1] = (b_pack[0] + b_y[1]) + (b_y[2] + b_y[3])
+    bz_move.start()
     hi, mid, lo = split3(wfull[w] / pt[...])
     wc_move.wait()
 
@@ -367,13 +371,12 @@
 
     ms_move = Transfer(range(1, NP), ms_copy)
     ms_move.start()
-    wy_move.start()
-
-    b_move.wait()
+
+    bz_move.wait()
     wt_move.wait()
     wt_row = lax.fori_loop(0, NP, lambda d, a: a + wt_part[d], jnp.zeros((1, 128), F32))
     wt_own = jnp.sum(jnp.where(lane == row, wt_row, 0.0), axis=1, keepdims=True)
-    packed = lax.fori_loop(1, NP, lambda d, a: a + b_recv[d], b_pack[...])
+    packed = sum([b_z[d] for d in range(1, 8)], b_pack[1])
     b_own = jnp.concatenate(
         [packed] + [pltpu.roll(packed, 128 - 32 * a, 1) for a in range(1, 4)], axis=0
     )
@@ -406,7 +409,7 @@
             for e in range(2):
                 k = 2 * j + e
                 f = x[k, :, lanes].astype(F32) - pe1[pl.ds(k, 1), lanes] - cols[e]
-                fs.append(jnp.where(cellw > 0.0, f, 0.0))
+                fs.append(f)
             for g in range(8):
                 s = slice(g * 8, g * 8 + 8)
                 pair = jnp.concatenate([fs[0][s], fs[1][s]], axis=0)
@@ -414,7 +417,7 @@
                 q_buf[g, at, lanes] = pair.astype(BF16)
                 u_buf[g, at, lanes] = wpair.astype(BF16)
 
-    loop(0, K // 2, r_pair)
+    loop(0, R_FIRST, r_pair)
 
     ms_move.wait()
     tile = lax.fori_loop(1, NP, lambda d, a: a + m_recv[d], m_stage[p])
@@ -428,18 +431,40 @@
     tile_of(w, p)[...] = tile
 
     def ma_copy(d):
-        return to_prod(tile_of(w, p), tile_of(w, p), ma_s.at[d], ma_r.at[d], prod_peer(d))
+        return to_prod(tile_of(w, p), tile_of(w, p), ma_s.at[d], ma_r.at[d], grid_peer(d, 1))
 
     def ma_arrived(d):
-        return to_prod(tile_of(w, p), tile_of(w, lax.rem(p + NP - d, NP)), ma_s.at[d], ma_r.at[d], prod_peer(d))
-
-    ma_move = Transfer(range(1, NP), ma_copy, ma_arrived)
-    ma_move.start()
+        return to_prod(tile_of(w, p), tile_of(w, grid_peer(d, -1)), ma_s.at[d], ma_r.at[d], grid_peer(d, 1))
+
+    def forward_tile(q):
+        for d in (2, 1, 3):
+            to_week(tile_of(w, q), tile_of(w, q), mx_s.at[d], mx_r.at[d], x_peer(d)).start()
+
+    near_first = sorted(
+        range(1, NP), key=lambda d: min(d // 8, 4 - d // 8) + min(d % 8, 8 - d % 8)
+    )
+    ma_move = Transfer(near_first, ma_copy, ma_arrived)
+    ma_move.start(near_first[::-1])
+    forward_tile(p)
+
+    for d in (1, 3, 2):
+        wy_move.wait((d,))
+        wd_move.start((d,))
 
     def r_dot(g, acc):
         return acc + lax.dot_general(u_buf[g], q_buf[g], NT, preferred_element_type=F32)
 
-    big = lax.fori_loop(0, 8, r_dot, jnp.zeros((K * 8, K * 8), F32))
+    def forward_tiles(ds):
+        for d in ds:
+            ma_move.wait((d,))
+            forward_tile(grid_peer(d, -1))
+
+    loop(R_FIRST, K // 2, r_pair)
+    big = lax.fori_loop(0, 5, r_dot, jnp.zeros((K * 8, K * 8), F32))
+    forward_tiles(near_first[:6])
+    big = lax.fori_loop(5, 7, r_dot, big)
+    forward_tiles(near_first[6:14])
+    big = r_dot(7, big)
     ri = lax.broadcasted_iota(jnp.int32, (K * 8, K * 8), 0)
     ci = lax.broadcasted_iota(jnp.int32, (K * 8, K * 8), 1)
     big = jnp.where(lax.rem(ri, 8) == lax.rem(ci, 8), big, 0.0)
@@ -459,7 +484,7 @@
     rw_move = Transfer(range(1, NW), rw_copy)
     rw_move.start()
 
-    ma_move.wait()
+    forward_tiles(near_first[14:])
 
     def rows_of(wk):
         return mm.at[pl.ds(pl.multiple_of(wk * WK, WK), WK)]
@@ -480,7 +505,7 @@
 
     mx_move = Transfer((1, 3, 2), mx_copy, mx_arrived)
     mc_move = Transfer((0, 1, 3, 2), mc_copy, mc_arrived)
-    mx_move.start()
+    mx_move.sent += [1, 3, 2]
     mc_move.start((0,))
 
     rw_move.wait()
@@ -497,9 +522,6 @@
     for d in (1, 3, 2):
         mx_move.wait((d,))
         mc_move.start((d,))
-    for d in (1, 3, 2):
-        wy_move.wait((d,))
-        wd_move.start((d,))
     wd_move.wait()
 
     def rest_to_bf16(i):
@@ -572,20 +594,17 @@
     gram_out[...] = ((r_rows + gram) / weight_total)[:, :K]
 
     for move in (
-        pt_move, ps_move, wt_move, wx_move, wc_move, wy_move, wd_move, pe_move, pf_move, b_move, ba_move,
+        pt_move, ps_move, wt_move, wx_move, wc_move, wy_move, wd_move, pe_move, pf_move, by_move, bz_move, ba_move,
         ms_move, ma_move, mx_move, mc_move, rw_move, rp_move,
     ):
         move.drain()
 
 
-def effects(x, weights, first, last):
+def effects(x, cell):
     vmem = pl.BlockSpec(memory_space=pltpu.VMEM)
     dma = pltpu.SemaphoreType.DMA
     scratch = [
         pltpu.VMEM((K, WK, PD), BF16),
-        pltpu.VMEM((WK, PD), jnp.int32),
-        pltpu.VMEM((PD,), jnp.int32),
-        pltpu.VMEM((PD,), jnp.int32),
         pltpu.VMEM((NW, WK, PD), F32),
         pltpu.VMEM((WEEKS, PD), BF16),
         pltpu.VMEM((1, PD), F32),
@@ -598,8 +617,9 @@
         pltpu.VMEM((NX, 8, HALF), F32),
         pltpu.VMEM((NW, 8, HALF), F32),
         pltpu.VMEM((K, PD), F32),
-        pltpu.VMEM((16, 128), F32),
-        pltpu.VMEM((NP, 16, 128), F32),
+        pltpu.VMEM((2, 16, 128), F32),
+        pltpu.VMEM((4, 16, 128), F32),
+        pltpu.VMEM((8, 16, 128), F32),
         pltpu.VMEM((NW, 32, 128), F32),
         pltpu.VMEM((NP, 8, 128), F32),
         pltpu.VMEM((NP, 8, 128), F32),
@@ -613,9 +633,9 @@
         pltpu.VMEM((NW, 8, 128), F32),
         pltpu.VMEM((NP, 8, 128), F32),
         pltpu.VMEM((WEEKS, 128), F32),
-        dma((7,)),
+        dma((4,)),
     ]
-    for n in (NX, NX, NP, NX, NX, len(W_PARTS) * NX, len(W_PARTS) * NX, NX, NX, NP, NW, NP, NP, NX, NX, NW, NP):
+    for n in (NX, NX, NP, NX, NX, len(W_PARTS) * NX, len(W_PARTS) * NX, NX, NX, 4, 8, NW, NP, NP, NX, NX, NW, NP):
         scratch += [dma((n,)), dma((n,))]
     return pl.pallas_call(
         effects_kernel,
@@ -624,59 +644,63 @@
             jax.ShapeDtypeStruct((WK, 128), F32),
             jax.ShapeDtypeStruct((K, K), F32),
         ),
-        in_specs=[pl.BlockSpec(memory_space=pl.ANY)] * 4,
+        in_specs=[pl.BlockSpec(memory_space=pl.ANY), vmem],
         out_specs=(vmem, vmem, vmem),
         scratch_shapes=scratch,
         compiler_params=pltpu.CompilerParams(
-            collective_id=0, has_side_effects=True, vmem_limit_bytes=48 * 2**20
+            collective_id=0, has_side_effects=True, vmem_limit_bytes=VMEM_LIMIT
         ),
         name="effects",
-    )(x, weights, first, last)
+    )(x, cell)
 
 
 KB = 4
 
 
-def output_kernel(x, first, last, pe4, we4, gram, out, gram_out):
-    w = lax.axis_index("week")
-    step = pl.program_id(0)
+def output_kernel(x, cell, pe4, we4, gram, out_hbm, gram_out, out, sem):
     gram_out[...] = gram[...]
     lane = lax.broadcasted_iota(jnp.int32, (WK, 128), 1)
-    ids = w * WK + lax.broadcasted_iota(jnp.int32, (WK, LC), 0)
-    cols = [
-        jnp.sum(jnp.where(lane == step * KB + e, we4[...], 0.0), axis=1, keepdims=True)
-        for e in range(KB)
-    ]
-    first_row = first[...].reshape(1, PD)
-    last_row = last[...].reshape(1, PD)
-    for c in range(PD // LC):
-        lanes = slice(c * LC, (c + 1) * LC)
-        live = (ids >= first_row[:, lanes]) & (ids <= last_row[:, lanes])
+
+    def copy(i):
+        rows = pl.ds(i * KB, KB)
+        return pltpu.make_async_copy(out.at[rows], out_hbm.at[rows], sem.at[i])
+
+    def block(i):
         for e in range(KB):
-            field = x[e, :, lanes].astype(F32) - pe4[pl.ds(step * KB + e, 1), lanes] - cols[e]
-            out[e, :, lanes] = jnp.where(live, field, 0.0).astype(BF16)
-
-
-def output(x, first, last, pe4, we4, gram):
+            k = i * KB + e
+            col = jnp.sum(jnp.where(lane == k, we4[...], 0.0), axis=1, keepdims=True)
+            for c in range(PD // LC):
+                lanes = slice(c * LC, (c + 1) * LC)
+                field = x[k, :, lanes].astype(F32) - pe4[pl.ds(k, 1), lanes] - col
+                out[k, :, lanes] = jnp.where(cell[:, lanes] > 0.0, field, 0.0).astype(BF16)
+        copy(i).start()
+
+    loop(0, K // KB, block)
+    loop(0, K // KB, lambda i: copy(i).wait())
+
+
+def output(x, cell, pe4, we4, gram):
     vmem = pl.BlockSpec(memory_space=pltpu.VMEM)
-    block = pl.BlockSpec((KB, WK, PD), lambda i: (i, 0, 0))
     return pl.pallas_call(
         output_kernel,
-        grid=(K // KB,),
         out_shape=(
             jax.ShapeDtypeStruct((K, WK, PD), BF16),
             jax.ShapeDtypeStruct((K, K), F32),
         ),
-        in_specs=[block, vmem, vmem, vmem, vmem, vmem],
-        out_specs=(block, vmem),
+        in_specs=[vmem] * 5,
+        out_specs=(pl.BlockSpec(memory_space=pl.ANY), vmem),
+        scratch_shapes=[pltpu.VMEM((K, WK, PD), BF16), pltpu.SemaphoreType.DMA((K // KB,))],
         compiler_params=pltpu.CompilerParams(vmem_limit_bytes=32 * 2**20),
         name="output",
-    )(x, first, last, pe4, we4, gram)
+    )(x, cell, pe4, we4, gram)
 
 
 def per_device(regressors, weights, first_week, last_week):
-    pe4, we4, gram = effects(regressors, weights, first_week, last_week)
-    return output(regressors, first_week, last_week, pe4, we4, gram)
+    ids = lax.axis_index("week") * WK + lax.broadcasted_iota(jnp.int32, (WK, PD), 0)
+    live = (ids >= first_week[None, :]) & (ids <= last_week[None, :])
+    cell = jnp.where(live, weights.astype(F32), 0.0)
+    pe4, we4, gram = effects(regressors, cell)
+    return output(regressors, cell, pe4, we4, gram)
 
 
 def solution(mesh):

time: 74.6 us -> 65.5 us (0.88)
  Pallas kernels: 70.9 us -> 63.4 us
  local copies, waits for them, and re-layouts: 2.77 us -> 0.01 us
  other arithmetic: 0 us -> 1.3 us
    pallas_call x1, Pallas kernels: 65.7 us -> 59.2 us  [effects(): pl.pallas_call(effects_kernel, out_shape=(jax.ShapeDtypeStruct((K, PD), F...]
    unnamed x8 -> x2, local copies, waits for them, and re-layouts: 2.77 us -> 0.01 us
    select_n x0 -> x1, other arithmetic: none -> 1.29 us  [per_device(): cell = jnp.where(live, weights.astype(F32), 0.0)]
    pallas_call x1, Pallas kernels: 5.26 us -> 4.16 us  [output(): pl.pallas_call(output_kernel, out_shape=(jax.ShapeDtypeStruct((K, WK, PD)...]
where the time goes in v3:
time: 65.5 us; the launch traced here: 65.4 us
  Pallas kernels  63.4 us (97%)
  other arithmetic  1.3 us (2%)
  between operations  0.67 us (1%)
    pallas_call x1, Pallas kernels, effects(): pl.pallas_call(effects_kernel, out_shape=(jax.ShapeDtypeStruct((K, PD), F...  59.2 us
    pallas_call x1, Pallas kernels, output(): pl.pallas_call(output_kernel, out_shape=(jax.ShapeDtypeStruct((K, WK, PD)...  4.16 us

profile of v3, /device:TPU:1, one launch (start us, length us, event | category | flops | bytes accessed | tf_op | source)
XLA Modules:
  0.0 65.4 jit_solution(16134707573682398390)
XLA Ops:
  0.6 0.0 copy-start
  0.7 1.3 %convert_select_fusion.cell_in.cell = f32[64,1536]{1,0:T(8,128)S(1)} fusion(s32[64,1536]{1,0:T(8,128)} %param.5, s32[1536]{0:T(1024)} %param.7, s32[1536]{0:T(1024)} %param.6, s32[64]{0:T(128)S(1)} %iota_add_fusion), kind=kLoop, calls=%fused_computation | loop fusion | flops 491520 | bytes 798976 | tf_op jit(solution)/shard_map/jit(_where)/select_n | solution.py:701
  2.0 59.2 %effects.1 = (f32[32,1536]{1,0:T(8,128)S(1)}, f32[64,128]{1,0:T(8,128)S(1)}, f32[32,32]{1,0:T(8,128)S(1)}) custom-call(bf16[32,64,1536]{2,1,0:T(8,128)(2,1)} %x.1, f32[64,1536]{1,0:T(8,128)S(1)} %convert_select_fusion.cell_in.cell), custom_call_target="tpu_custom_call" | custom-call | tf_op jit(solution)/shard_map/effects/pallas_call | solution.py:640
  61.2 0.0 copy-done
  61.2 4.2 %output.1 = (bf16[32,64,1536]{2,1,0:T(8,128)(2,1)}, f32[32,32]{1,0:T(8,128)}) custom-call(bf16[32,64,1536]{2,1,0:T(8,128)(2,1)S(1)} %copy-done, f32[64,1536]{1,0:T(8,128)S(1)} %convert_select_fusion.cell_in.cell, f32[32,1536]{1,0:T(8,128)S(1)} %get-tuple-element.5.pe4, f32[64,128]{1,0:T(8,128)S(1)} %get-tuple-element.6.we4, f32[32,32]{1,0:T(8,128)S(1)} %get-tuple-element.7.gram), custom_call_target="tpu_custom_call" | custom-call | tf_op jit(solution)/shard_map/output/pallas_call | solution.py:684
  (1 shorter events, 0.0 us)
Async XLA Ops:
  0.6 60.6 %copy-start = (bf16[32,64,1536]{2,1,0:T(8,128)(2,1)S(1)}, bf16[32,64,1536]{2,1,0:T(8,128)(2,1)}, u32[]{:S(2)}) copy-start(bf16[32,64,1536]{2,1,0:T(8,128)(2,1)} %x.1) | copy-start | bytes 18874372

commit v4 on v3

--- a/solution.py
+++ b/solution.py
@@ -23,8 +23,8 @@
 WEEKS = NW * WK
 LC = 384
 HALF = PD // 2
-W_PARTS = (0, 16, 40, 64)
-R_FIRST = 8
+W_PARTS = (0, 8, 40, 64)
+R_FIRST = 4
 VMEM_LIMIT = 53 * 2**20
 
 
@@ -73,10 +73,10 @@
 def effects_kernel(
     x_hbm, cell_in,
     pe4_out, we4_out, gram_out,
-    x, wfull, wb, pt_own, pt_sib, pt_all, pt, wt_part, ps_stage, ps_sib, ps_recv, pe1_chunks, pe1,
+    x, wfull, wb, pt_own, pt_sib, pt_all, pt, ps_stage, ps_sib, ps_recv, pe1_chunks, pe1,
     b_pack, b_y, b_z, b_all, m_stage, m_recv, mm, m_hi, m_mid, m_lo,
     q_buf, u_buf, r_pack, r_week, r_prod, we_buf,
-    x_sem, pt_s, pt_r, ps_s, ps_r, wt_s, wt_r, pe_s, pe_r, pf_s, pf_r, wx_s, wx_r, wc_s, wc_r, wy_s, wy_r, wd_s, wd_r,
+    x_sem, ready, pt_s, pt_r, ps_s, ps_r, pe_s, pe_r, pf_s, pf_r, wx_s, wx_r, wc_s, wc_r, wy_s, wy_r, wd_s, wd_r,
     by_s, by_r, bz_s, bz_r, ba_s, ba_r, ms_s, ms_r, ma_s, ma_r, mx_s, mx_r, mc_s, mc_r,
     rw_s, rw_r, rp_s, rp_r,
 ):
@@ -127,11 +127,12 @@
     def greet_week(d):
         pl.semaphore_signal(barrier, inc=1, device_id={"week": week_peer(d)}, device_id_type=MESH)
 
-    def greet_prod(d):
-        pl.semaphore_signal(barrier, inc=1, device_id={"prod": prod_peer(d)}, device_id_type=MESH)
+    def greet_grid(d):
+        pl.semaphore_signal(barrier, inc=1, device_id={"prod": grid_peer(d, 1)}, device_id_type=MESH)
 
     loop(1, NW, greet_week)
-    loop(1, NP, greet_prod)
+    loop(1, 4, lambda d: greet_grid(8 * d))
+    loop(1, 8, greet_grid)
 
     cell = cell_in[...]
     wfull[w] = cell
@@ -140,7 +141,7 @@
     lane = lax.broadcasted_iota(jnp.int32, (WK, 128), 1)
     row = lax.broadcasted_iota(jnp.int32, (WK, 128), 0)
     wt_col = jnp.sum(cell, axis=1, keepdims=True)
-    wt_part[p] = jnp.sum(jnp.where(lane == row, wt_col, 0.0), axis=0, keepdims=True)
+    wt_local = jnp.sum(jnp.where(lane == row, wt_col, 0.0), axis=0, keepdims=True)
 
     def sums_group(g, acc):
         x_copy(g).wait()
@@ -157,11 +158,16 @@
                     part = part + weighted[:, t * 128:(t + 1) * 128]
             return acc + jnp.where(lane == k, jnp.sum(part, axis=1, keepdims=True), 0.0)
 
-        return lax.fori_loop(0, 8, one, acc, unroll=2)
+        return lax.fori_loop(0, 8, one, acc, unroll=8)
 
     ws = lax.fori_loop(0, 4, sums_group, jnp.zeros((WK, 128), F32))
 
-    pl.semaphore_wait(barrier, NW - 1 + NP - 1)
+    pl.semaphore_wait(barrier, NW - 1 + 3 + 7)
+
+    def pass_on(d):
+        pl.semaphore_signal(ready, inc=1, device_id={"prod": grid_peer(d, 1)}, device_id_type=MESH)
+
+    loop(1, 8, pass_on)
 
     def pt_copy(d):
         if d == 0:
@@ -183,12 +189,6 @@
     ps_move = Transfer((0, 2, 1, 3), ps_copy)
     pt_move.start((0,))
     ps_move.start((0,))
-
-    def wt_copy(d):
-        return to_prod(wt_part.at[p], wt_part.at[p], wt_s.at[d], wt_r.at[d], prod_peer(d))
-
-    def wt_arrived(d):
-        return to_prod(wt_part.at[p], wt_part.at[lax.rem(p + NP - d, NP)], wt_s.at[d], wt_r.at[d], prod_peer(d))
 
     def first_half(chip, other):
         return jnp.where(chip < other, 0, 1)
@@ -249,8 +249,6 @@
         here = half_of(other_core(x_from(d)), 1 - first_half(xi, chip_from(d)))
         return to_week(here, here, wd_s.at[d], wd_r.at[d], sib)
 
-    wt_move = Transfer(range(1, NP), wt_copy, wt_arrived)
-    wt_move.start()
     parts = range(len(W_PARTS) - 1)
     wx_move = Transfer([d + NX * e for e in parts for d in (2, 1, 3)], wx_copy, wx_arrived)
     wc_move = Transfer([0] + [d + NX * e for e in parts for d in (1, 3, 2)], wc_copy, wc_arrived)
@@ -323,9 +321,10 @@
     taken = lax.dot_general(own_wb, pe_rows, NT, preferred_element_type=F32)
     taken = taken + (pltpu.roll(taken, 128 - K, 1) + pltpu.roll(taken, 128 - 2 * K, 1))
     bt = jnp.where(lane < K, ws - taken, 0.0)
-    b_pack[0] = sum(
+    packed = sum(
         [pltpu.roll(bt[16 * a:16 * a + 16], 32 * a, 1) for a in range(1, 4)], bt[:16]
     )
+    b_pack[0] = jnp.concatenate([packed, jnp.broadcast_to(wt_local, (8, 128))], axis=0)
 
     def by_copy(d):
         return to_prod(b_pack.at[0], b_y.at[d], by_s.at[d], by_r.at[d], grid_peer(8 * d, 1))
@@ -370,13 +369,13 @@
         return to_prod(m_stage.at[q], m_recv.at[d], ms_s.at[d], ms_r.at[d], q)
 
     ms_move = Transfer(range(1, NP), ms_copy)
+    pl.semaphore_wait(ready, 7)
     ms_move.start()
 
     bz_move.wait()
-    wt_move.wait()
-    wt_row = lax.fori_loop(0, NP, lambda d, a: a + wt_part[d], jnp.zeros((1, 128), F32))
-    wt_own = jnp.sum(jnp.where(lane == row, wt_row, 0.0), axis=1, keepdims=True)
     packed = sum([b_z[d] for d in range(1, 8)], b_pack[1])
+    wt_own = jnp.sum(jnp.where(lane == row, packed[16:17], 0.0), axis=1, keepdims=True)
+    packed = packed[:16]
     b_own = jnp.concatenate(
         [packed] + [pltpu.roll(packed, 128 - 32 * a, 1) for a in range(1, 4)], axis=0
     )
@@ -594,7 +593,7 @@
     gram_out[...] = ((r_rows + gram) / weight_total)[:, :K]
 
     for move in (
-        pt_move, ps_move, wt_move, wx_move, wc_move, wy_move, wd_move, pe_move, pf_move, by_move, bz_move, ba_move,
+        pt_move, ps_move, wx_move, wc_move, wy_move, wd_move, pe_move, pf_move, by_move, bz_move, ba_move,
         ms_move, ma_move, mx_move, mc_move, rw_move, rp_move,
     ):
         move.drain()
@@ -611,15 +610,14 @@
         pltpu.VMEM((1, PD), F32),
         pltpu.VMEM((NX, 1, PD), F32),
         pltpu.VMEM((1, PD), F32),
-        pltpu.VMEM((NP, 1, 128), F32),
         pltpu.VMEM((2, NX, 8, HALF), F32),
         pltpu.VMEM((NX, 8, HALF), F32),
         pltpu.VMEM((NX, 8, HALF), F32),
         pltpu.VMEM((NW, 8, HALF), F32),
         pltpu.VMEM((K, PD), F32),
-        pltpu.VMEM((2, 16, 128), F32),
-        pltpu.VMEM((4, 16, 128), F32),
-        pltpu.VMEM((8, 16, 128), F32),
+        pltpu.VMEM((2, 24, 128), F32),
+        pltpu.VMEM((4, 24, 128), F32),
+        pltpu.VMEM((8, 24, 128), F32),
         pltpu.VMEM((NW, 32, 128), F32),
         pltpu.VMEM((NP, 8, 128), F32),
         pltpu.VMEM((NP, 8, 128), F32),
@@ -634,8 +632,9 @@
         pltpu.VMEM((NP, 8, 128), F32),
         pltpu.VMEM((WEEKS, 128), F32),
         dma((4,)),
+        pltpu.SemaphoreType.REGULAR,
     ]
-    for n in (NX, NX, NP, NX, NX, len(W_PARTS) * NX, len(W_PARTS) * NX, NX, NX, 4, 8, NW, NP, NP, NX, NX, NW, NP):
+    for n in (NX, NX, NX, NX, len(W_PARTS) * NX, len(W_PARTS) * NX, NX, NX, 4, 8, NW, NP, NP, NX, NX, NW, NP):
         scratch += [dma((n,)), dma((n,))]
     return pl.pallas_call(
         effects_kernel,

time: 65.5 us -> 63.4 us (0.968)
  Pallas kernels: 63.4 us -> 61.4 us
    pallas_call x1, Pallas kernels: 59.2 us -> 57.2 us  [effects(): pl.pallas_call(effects_kernel, out_shape=(jax.ShapeDtypeStruct((K, PD), F...]
where the time goes in v4:
time: 63.4 us
  Pallas kernels  61.4 us (97%)
  other arithmetic  1.3 us (2%)
  between operations  0.67 us (1%)
    pallas_call x1, Pallas kernels, effects(): pl.pallas_call(effects_kernel, out_shape=(jax.ShapeDtypeStruct((K, PD), F...  57.2 us
    pallas_call x1, Pallas kernels, output(): pl.pallas_call(output_kernel, out_shape=(jax.ShapeDtypeStruct((K, WK, PD)...  4.16 us
    select_n x1, other arithmetic, per_device(): cell = jnp.where(live, weights.astype(F32), 0.0)  1.29 us

profile of v4, /device:TPU:1, one launch (start us, length us, event | category | flops | bytes accessed | tf_op | source)
XLA Modules:
  0.0 63.4 jit_solution(6768686212316234064)
XLA Ops:
  0.6 0.0 copy-start
  0.7 1.3 %convert_select_fusion.cell_in.cell = f32[64,1536]{1,0:T(8,128)S(1)} fusion(s32[64,1536]{1,0:T(8,128)} %param.5, s32[1536]{0:T(1024)} %param.7, s32[1536]{0:T(1024)} %param.6, s32[64]{0:T(128)S(1)} %iota_add_fusion), kind=kLoop, calls=%fused_computation | loop fusion | flops 491520 | bytes 798976 | tf_op jit(solution)/shard_map/jit(_where)/select_n | solution.py:700
  2.0 57.2 %effects.1 = (f32[32,1536]{1,0:T(8,128)S(1)}, f32[64,128]{1,0:T(8,128)S(1)}, f32[32,32]{1,0:T(8,128)S(1)}) custom-call(bf16[32,64,1536]{2,1,0:T(8,128)(2,1)} %x.1, f32[64,1536]{1,0:T(8,128)S(1)} %convert_select_fusion.cell_in.cell), custom_call_target="tpu_custom_call" | custom-call | tf_op jit(solution)/shard_map/effects/pallas_call | solution.py:639
  59.2 0.0 copy-done
  59.2 4.2 %output.1 = (bf16[32,64,1536]{2,1,0:T(8,128)(2,1)}, f32[32,32]{1,0:T(8,128)}) custom-call(bf16[32,64,1536]{2,1,0:T(8,128)(2,1)S(1)} %copy-done, f32[64,1536]{1,0:T(8,128)S(1)} %convert_select_fusion.cell_in.cell, f32[32,1536]{1,0:T(8,128)S(1)} %get-tuple-element.5.pe4, f32[64,128]{1,0:T(8,128)S(1)} %get-tuple-element.6.we4, f32[32,32]{1,0:T(8,128)S(1)} %get-tuple-element.7.gram), custom_call_target="tpu_custom_call" | custom-call | tf_op jit(solution)/shard_map/output/pallas_call | solution.py:683
  (1 shorter events, 0.0 us)
Async XLA Ops:
  0.6 58.6 %copy-start = (bf16[32,64,1536]{2,1,0:T(8,128)(2,1)S(1)}, bf16[32,64,1536]{2,1,0:T(8,128)(2,1)}, u32[]{:S(2)}) copy-start(bf16[32,64,1536]{2,1,0:T(8,128)(2,1)} %x.1) | copy-start | bytes 18874372

commit v5 on v4

--- a/solution.py
+++ b/solution.py
@@ -24,7 +24,7 @@
 LC = 384
 HALF = PD // 2
 W_PARTS = (0, 8, 40, 64)
-R_FIRST = 4
+R_FIRST = 10
 VMEM_LIMIT = 53 * 2**20
 
 
@@ -160,7 +160,7 @@
 
         return lax.fori_loop(0, 8, one, acc, unroll=8)
 
-    ws = lax.fori_loop(0, 4, sums_group, jnp.zeros((WK, 128), F32))
+    ws = lax.fori_loop(0, 3, sums_group, jnp.zeros((WK, 128), F32))
 
     pl.semaphore_wait(barrier, NW - 1 + 3 + 7)
 
@@ -188,7 +188,6 @@
     pt_move = Transfer((0, 2, 1, 3), pt_copy, pt_arrived)
     ps_move = Transfer((0, 2, 1, 3), ps_copy)
     pt_move.start((0,))
-    ps_move.start((0,))
 
     def first_half(chip, other):
         return jnp.where(chip < other, 0, 1)
@@ -259,6 +258,8 @@
         wx_move.start([d + NX * e for d in (2, 1, 3)])
 
     send_part(0)
+    ws = lax.fori_loop(3, 4, sums_group, ws)
+    ps_move.start((0,))
     pt_move.wait((0,))
     pt_all[xi] = pt_own[...] + pt_sib[...]
     ps_move.wait((0,))

time: 63.4 us -> 62.2 us (0.981)
  Pallas kernels: 61.4 us -> 60.1 us
    pallas_call x1, Pallas kernels: 57.2 us -> 56 us  [effects(): pl.pallas_call(effects_kernel, out_shape=(jax.ShapeDtypeStruct((K, PD), F...]
where the time goes in v5:
time: 62.2 us; the launch traced here: 62.1 us
  Pallas kernels  60.1 us (97%)
  other arithmetic  1.3 us (2%)
  between operations  0.67 us (1%)
    pallas_call x1, Pallas kernels, effects(): pl.pallas_call(effects_kernel, out_shape=(jax.ShapeDtypeStruct((K, PD), F...  56 us
    pallas_call x1, Pallas kernels, output(): pl.pallas_call(output_kernel, out_shape=(jax.ShapeDtypeStruct((K, WK, PD)...  4.16 us
    select_n x1, other arithmetic, per_device(): cell = jnp.where(live, weights.astype(F32), 0.0)  1.29 us

profile of v5, /device:TPU:1, one launch (start us, length us, event | category | flops | bytes accessed | tf_op | source)
XLA Modules:
  0.0 62.1 jit_solution(15892469072253121442)
XLA Ops:
  0.6 0.0 copy-start
  0.7 1.3 %convert_select_fusion.cell_in.cell = f32[64,1536]{1,0:T(8,128)S(1)} fusion(s32[64,1536]{1,0:T(8,128)} %param.5, s32[1536]{0:T(1024)} %param.7, s32[1536]{0:T(1024)} %param.6, s32[64]{0:T(128)S(1)} %iota_add_fusion), kind=kLoop, calls=%fused_computation | loop fusion | flops 491520 | bytes 798976 | tf_op jit(solution)/shard_map/jit(_where)/select_n | solution.py:701
  2.0 56.0 %effects.1 = (f32[32,1536]{1,0:T(8,128)S(1)}, f32[64,128]{1,0:T(8,128)S(1)}, f32[32,32]{1,0:T(8,128)S(1)}) custom-call(bf16[32,64,1536]{2,1,0:T(8,128)(2,1)} %x.1, f32[64,1536]{1,0:T(8,128)S(1)} %convert_select_fusion.cell_in.cell), custom_call_target="tpu_custom_call" | custom-call | tf_op jit(solution)/shard_map/effects/pallas_call | solution.py:640
  57.9 0.0 copy-done
  57.9 4.2 %output.1 = (bf16[32,64,1536]{2,1,0:T(8,128)(2,1)}, f32[32,32]{1,0:T(8,128)}) custom-call(bf16[32,64,1536]{2,1,0:T(8,128)(2,1)S(1)} %copy-done, f32[64,1536]{1,0:T(8,128)S(1)} %convert_select_fusion.cell_in.cell, f32[32,1536]{1,0:T(8,128)S(1)} %get-tuple-element.5.pe4, f32[64,128]{1,0:T(8,128)S(1)} %get-tuple-element.6.we4, f32[32,32]{1,0:T(8,128)S(1)} %get-tuple-element.7.gram), custom_call_target="tpu_custom_call" | custom-call | tf_op jit(solution)/shard_map/output/pallas_call | solution.py:684
  (1 shorter events, 0.0 us)
Async XLA Ops:
  0.6 57.3 %copy-start = (bf16[32,64,1536]{2,1,0:T(8,128)(2,1)S(1)}, bf16[32,64,1536]{2,1,0:T(8,128)(2,1)}, u32[]{:S(2)}) copy-start(bf16[32,64,1536]{2,1,0:T(8,128)(2,1)} %x.1) | copy-start | bytes 18874372
